TPU v7x, 512 devices: a whole 4x4x16 slice. The times are simulated.
512 devices in a mesh: dp: 8 (over y, core), ctx: 32 (over z, x_hi), tp: 2 (over x_lo).
Axes of the slice: x: 4 (x_hi: 2, x_lo: 2; x = x_hi * 2 + x_lo), y: 4, z: 16, core: 2. Of those that a mesh axis runs over, the one named last changes fastest.
Arguments:
- query_states: bfloat16 [8, 4096, 1024], P('dp', 'ctx', 'tp'), may hold values from -9 to 9
- key_states: bfloat16 [8, 4096, 1024], P('dp', 'ctx', 'tp'), may hold values from -9 to 9
- value_states: bfloat16 [8, 4096, 1024], P('dp', 'ctx', 'tp'), may hold values from -6 to 6
- out_weight: bfloat16 [2048, 1024], P('ctx', 'tp'), may hold values from -1.5 to 1.5
- grad_output: bfloat16 [8, 4096, 2048], P('dp', 'ctx', 'tp'), may hold values from -0.625 to 0.625
- segment_table: int32 [8, 3, 5], P('dp'), may hold values from 0 to 4095, as said below
Outputs:
- layer_output: bfloat16 [8, 4096, 2048], P('dp', 'ctx', 'tp')
- grad_queries: bfloat16 [8, 4096, 1024], P('dp', 'ctx', 'tp')
- grad_keys: bfloat16 [8, 4096, 1024], P('dp', 'ctx', 'tp')
- grad_values: bfloat16 [8, 4096, 1024], P('dp', 'ctx', 'tp')
- grad_weight: float32 [2048, 1024], P('ctx', 'tp')
Inputs may be any that keep to these rules, and one draw needn't show every extreme that they name: `segment_table`: row 0 holds the starts, row 1 the lengths and row 2 the flags (1 for an image, 0 for text) of 5 segments that tile the document in order. Text and image segments alternate, beginning and ending with text; every text segment has one token or more, the last text segment exactly one, and every image segment exactly 1024.
All inputs are finite; a program needn't handle non-finite values.
Results may differ from a plain program's by a relative error of at most 0.027.
Values may be sent and summed in bfloat16 or wider, within the bound.
A program may use at most 64 MiB of HBM per device.

v0:
```python
import jax
import jax.numpy as jnp
from jax import lax
from jax.sharding import PartitionSpec as P

HS = 64


NEG_FILL = -1e30


def from_partner(shard, axis, bit):
    return lax.ppermute(shard, axis, [(i, i ^ 1 << bit) for i in range(lax.axis_size(axis))])


def reach_of(seg_table, positions):
    seg_starts = seg_table[0]
    seg_ends = seg_table[0] + seg_table[1]
    is_image = seg_table[2] == 1
    inside = (positions[:, None] >= seg_starts[None, :]) & (positions[:, None] < seg_ends[None, :])
    image_hit = inside & is_image[None, :]
    image_last = jnp.sum(jnp.where(image_hit, seg_ends[None, :] - 1, 0), axis=1)
    return jnp.where(jnp.any(image_hit, axis=1), image_last, positions)


def tile_scores(query_rows, tile_keys, score_scale):
    return score_scale * lax.dot_general(
        query_rows, tile_keys, (((1,), (1,)), ((), ())), preferred_element_type=jnp.float32
    )


def tile_allowed(tile_index, tile_size, key_reach):
    offsets = tile_index * tile_size + jnp.arange(tile_size, dtype=jnp.int32)
    return offsets[None, :] <= key_reach[:, None]


def forward_block(query_rows, key_reach, keys_all, values_all, tile_size, score_scale):
    row_count = query_rows.shape[0]
    tile_count = jnp.max(key_reach) // tile_size + 1

    def collect_stats(tile_index, running):
        row_top, row_total = running
        tile_keys = lax.dynamic_slice_in_dim(keys_all, tile_index * tile_size, tile_size, 0)
        allowed = tile_allowed(tile_index, tile_size, key_reach)
        scores = jnp.where(allowed, tile_scores(query_rows, tile_keys, score_scale), NEG_FILL)
        new_top = jnp.maximum(row_top, jnp.max(scores, axis=1))
        exp_terms = jnp.where(allowed, jnp.exp(scores - new_top[:, None]), 0.0)
        return (new_top, row_total * jnp.exp(row_top - new_top) + jnp.sum(exp_terms, axis=1))

    start_state = (
        jnp.full((row_count,), NEG_FILL, jnp.float32),
        jnp.zeros((row_count,), jnp.float32),
    )
    row_top, row_total = lax.fori_loop(0, tile_count, collect_stats, start_state)
    log_total = row_top + jnp.log(row_total)

    def collect_out(tile_index, summed):
        tile_keys = lax.dynamic_slice_in_dim(keys_all, tile_index * tile_size, tile_size, 0)
        tile_values = lax.dynamic_slice_in_dim(values_all, tile_index * tile_size, tile_size, 0)
        allowed = tile_allowed(tile_index, tile_size, key_reach)
        scores = jnp.where(allowed, tile_scores(query_rows, tile_keys, score_scale), NEG_FILL)
        prob_tile = jnp.where(allowed, jnp.exp(scores - log_total[:, None]), 0.0).astype(
            jnp.bfloat16
        )
        return summed + jnp.dot(prob_tile, tile_values, preferred_element_type=jnp.float32)

    summed = lax.fori_loop(
        0, tile_count, collect_out, jnp.zeros((row_count, values_all.shape[1]), jnp.float32)
    )
    return (summed.astype(jnp.bfloat16), log_total)


def backward_block(grads_pairs, block_items, keys_all, values_all, tile_size, score_scale):
    query_rows, key_reach, grad_rows, row_delta, log_total = block_items
    tile_count = jnp.max(key_reach) // tile_size + 1

    def collect_grads(tile_index, running):
        grad_query, grads_acc = running
        tile_begin = tile_index * tile_size
        tile_keys = lax.dynamic_slice_in_dim(keys_all, tile_begin, tile_size, 0)
        tile_values = lax.dynamic_slice_in_dim(values_all, tile_begin, tile_size, 0)
        allowed = tile_allowed(tile_index, tile_size, key_reach)
        scores = jnp.where(allowed, tile_scores(query_rows, tile_keys, score_scale), NEG_FILL)
        prob_tile = jnp.where(allowed, jnp.exp(scores - log_total[:, None]), 0.0)
        grad_probs = lax.dot_general(
            grad_rows, tile_values, (((1,), (1,)), ((), ())), preferred_element_type=jnp.float32
        )
        grad_scores = (prob_tile * (grad_probs - row_delta[:, None])).astype(jnp.bfloat16)
        grad_query = grad_query + score_scale * jnp.dot(
            grad_scores, tile_keys, preferred_element_type=jnp.float32
        )
        key_part = score_scale * lax.dot_general(
            grad_scores, query_rows, (((0,), (0,)), ((), ())), preferred_element_type=jnp.float32
        )
        value_part = lax.dot_general(
            prob_tile.astype(jnp.bfloat16),
            grad_rows,
            (((0,), (0,)), ((), ())),
            preferred_element_type=jnp.float32,
        )
        current = lax.dynamic_slice_in_dim(grads_acc, tile_begin, tile_size, 0)
        grads_acc = lax.dynamic_update_slice_in_dim(
            grads_acc, current + jnp.concatenate([key_part, value_part], axis=1), tile_begin, 0
        )
        return (grad_query, grads_acc)

    start_state = (jnp.zeros(query_rows.shape, jnp.float32), grads_pairs)
    grad_query, grads_pairs = lax.fori_loop(0, tile_count, collect_grads, start_state)
    return (grads_pairs, grad_query.astype(jnp.bfloat16))


def body(query_states, key_states, value_states, out_weight, grad_output, segment_table):
    ctx_size = lax.axis_size("ctx")
    tokens_here = query_states.shape[1]
    width_tp = query_states.shape[2]
    heads_here = width_tp // HS
    group_size = ctx_size // heads_here
    sub_rows = tokens_here // group_size
    seq_len = tokens_here * ctx_size
    query_count = ctx_size * sub_rows
    member = lax.axis_index("ctx") % group_size
    score_scale = HS ** (-0.5)
    query_local = query_states[0]
    pair_local = jnp.concatenate(
        [
            key_states[0].reshape(tokens_here, heads_here, HS),
            value_states[0].reshape(tokens_here, heads_here, HS),
        ],
        axis=2,
    )

    def to_heads(matrix):
        col_width = matrix.shape[1] // heads_here
        return (
            matrix.reshape(group_size, sub_rows, heads_here, col_width)
            .transpose(2, 0, 1, 3)
            .reshape(ctx_size, sub_rows, col_width)
        )

    def from_heads(blocks):
        col_width = blocks.shape[2]
        return (
            blocks.reshape(heads_here, group_size, sub_rows, col_width)
            .transpose(1, 2, 0, 3)
            .reshape(tokens_here, heads_here * col_width)
        )

    query_heads, pair_heads = (
        lax.all_to_all(to_heads(query_local), "ctx", split_axis=0, concat_axis=0, tiled=True),
        lax.all_to_all(
            to_heads(pair_local.reshape(tokens_here, heads_here * 2 * HS)),
            "ctx",
            split_axis=0,
            concat_axis=0,
            tiled=True,
        ),
    )
    collected = pair_heads[None]
    for bit_index in range(group_size.bit_length() - 1):
        partner = from_partner(collected, "ctx", bit_index)
        upper_half = member // 2**bit_index % 2 == 1
        collected = jnp.where(
            upper_half,
            jnp.concatenate([partner, collected], axis=0),
            jnp.concatenate([collected, partner], axis=0),
        )
    pairs_all = collected.transpose(1, 0, 2, 3).reshape(seq_len, 2 * HS)
    keys_all = pairs_all[:, :HS]
    values_all = pairs_all[:, HS:]
    query_pos = (
        jnp.arange(ctx_size, dtype=jnp.int32)[:, None] * tokens_here
        + member * sub_rows
        + jnp.arange(sub_rows, dtype=jnp.int32)[None, :]
    ).reshape(query_count)
    key_reach = reach_of(segment_table[0], query_pos)
    block_rows = 512
    block_count = query_count // block_rows
    tile_size = 512
    query_flat = query_heads.reshape(query_count, HS)

    def run_forward(block_items):
        return forward_block(
            block_items[0], block_items[1], keys_all, values_all, tile_size, score_scale
        )

    out_blocks, log_blocks = lax.map(
        run_forward,
        (
            query_flat.reshape(block_count, block_rows, HS),
            key_reach.reshape(block_count, block_rows),
        ),
    )
    out_heads = out_blocks.reshape(ctx_size, sub_rows, HS)
    attn_local = from_heads(
        lax.all_to_all(out_heads, "ctx", split_axis=0, concat_axis=0, tiled=True)
    )
    weight_full = lax.all_gather(out_weight, "ctx", axis=0, tiled=True)
    partial_out = lax.dot_general(
        attn_local, weight_full, (((1,), (1,)), ((), ())), preferred_element_type=jnp.float32
    )
    mixed_out = lax.psum_scatter(
        partial_out.astype(jnp.bfloat16), "tp", scatter_dimension=1, tiled=True
    )
    grad_full = lax.all_gather(grad_output[0], "tp", axis=1, tiled=True)
    grad_attn = jnp.dot(grad_full, weight_full, preferred_element_type=jnp.float32)
    grad_attn = grad_attn.astype(jnp.bfloat16)
    weight_part = lax.psum_scatter(
        lax.dot_general(
            grad_full, attn_local, (((0,), (0,)), ((), ())), preferred_element_type=jnp.float32
        ).astype(jnp.bfloat16),
        "ctx",
        scatter_dimension=0,
        tiled=True,
    )
    grad_weight = lax.psum(weight_part, "dp").astype(jnp.float32)
    grad_heads = lax.all_to_all(
        to_heads(grad_attn), "ctx", split_axis=0, concat_axis=0, tiled=True
    ).reshape(query_count, HS)
    row_delta = jnp.sum(
        grad_heads.astype(jnp.float32) * out_blocks.reshape(query_count, HS).astype(jnp.float32),
        axis=1,
    )

    def run_backward(grads_pairs, block_items):
        return backward_block(
            grads_pairs, block_items, keys_all, values_all, tile_size, score_scale
        )

    back_items = (
        query_flat.reshape(block_count, block_rows, HS),
        key_reach.reshape(block_count, block_rows),
        grad_heads.reshape(block_count, block_rows, HS),
        row_delta.reshape(block_count, block_rows),
        log_blocks,
    )
    grads_pairs, grad_query = lax.scan(
        run_backward, jnp.zeros((seq_len, 2 * HS), jnp.float32), back_items
    )
    grad_query = grad_query.reshape(ctx_size, sub_rows, HS)
    shares = grads_pairs.reshape(ctx_size, group_size, sub_rows, 2 * HS).transpose(1, 0, 2, 3)
    for bit_index in reversed(range(group_size.bit_length() - 1)):
        half_size = shares.shape[0] // 2
        upper_half = member // 2**bit_index % 2 == 1
        kept_part = jnp.where(upper_half, shares[half_size:], shares[:half_size])
        sent_part = jnp.where(upper_half, shares[:half_size], shares[half_size:])
        shares = kept_part + from_partner(sent_part.astype(jnp.bfloat16), "ctx", bit_index).astype(
            sent_part.dtype
        )
    query_back, pair_back = (
        lax.all_to_all(grad_query, "ctx", split_axis=0, concat_axis=0, tiled=True),
        lax.all_to_all(
            shares[0].astype(jnp.bfloat16), "ctx", split_axis=0, concat_axis=0, tiled=True
        ),
    )
    query_grads = from_heads(query_back)
    pair_grads = from_heads(pair_back).reshape(tokens_here, heads_here, 2 * HS)
    grad_keys = pair_grads[:, :, :HS].reshape(tokens_here, width_tp)
    grad_values = pair_grads[:, :, HS:].reshape(tokens_here, width_tp)
    return (mixed_out[None], query_grads[None], grad_keys[None], grad_values[None], grad_weight)


def solution(mesh):
    placed = (
        P("dp", "ctx", "tp"),
        P("dp", "ctx", "tp"),
        P("dp", "ctx", "tp"),
        P("ctx", "tp"),
        P("dp", "ctx", "tp"),
        P("dp", None, None),
    )
    return jax.shard_map(
        body,
        mesh=mesh,
        in_specs=placed,
        out_specs=(
            P("dp", "ctx", "tp"),
            P("dp", "ctx", "tp"),
            P("dp", "ctx", "tp"),
            P("dp", "ctx", "tp"),
            P("ctx", "tp"),
        ),
        check_vma=False,
    )
```

profile of v0, /device:TPU:1, one launch (start us, length us, event | category | flops | bytes accessed | tf_op | source)
XLA Modules:
  0.0 987.2 jit_solution(10295377537934736459)
XLA Ops:
  10.3 18.5 %all-to-all-start.1 = ((bf16[32,32,128]{2,1,0:T(8,128)(2,1)}), bf16[32,32,128]{2,1,0:T(8,128)(2,1)S(1)}, u32[]{:S(2)}, u32[]{:S(2)}) async-start(bf16[32,32,128]{2,1,0:T(8,128)(2,1)} %bitcast.21), calls=%async_computation.1 | async-start | bytes 524288 | tf_op jit(solution)/shard_map/all_to_all | solution.py:150
  30.7 18.9 %all-to-all-done.1 = bf16[32,32,128]{2,1,0:T(8,128)(2,1)S(1)} async-done(((bf16[32,32,128]{2,1,0:T(8,128)(2,1)}), bf16[32,32,128]{2,1,0:T(8,128)(2,1)S(1)}, u32[]{:S(2)}, u32[]{:S(2)}) %all-to-all-start.1) | async-done | bytes 262176 | tf_op jit(solution)/shard_map/all_to_all | solution.py:150
  49.6 5.2 all-to-all-start
  54.8 4.6 collective-permute-start
  59.5 5.5 collective-permute-done
  65.1 2.9 collective-permute-start.1
  70.0 9.3 collective-permute-done.1
  79.7 24.8 %while.95 = (s32[]{:T(128)}, bf16[2,512,64]{1,2,0:T(8,128)(2,1)S(1)}, f32[2,512]{1,0:T(2,128)}, s32[2,512]{1,0:T(2,128)S(1)}, bf16[2,512,64]{2,1,0:T(8,128)(2,1)...) while((s32[]{:T(128)}, ...), condition=%wide.region_10.11_spmd, body=%wide.region_2.10_spmd.sunk | while | flops 104401952 | bytes 3538849 | solution.py:186
  83.0 2.6 while.98
  87.0 2.6 while.99
  92.9 5.2 while.98
  99.4 5.2 while.99
  105.6 14.0 %all-to-all-start.2 = ((bf16[32,2,1024]{2,1,0:T(2,128)(2,1)}), bf16[32,2,1024]{2,1,0:T(2,128)(2,1)S(1)}, u32[]{:S(2)}, u32[]{:S(2)}) async-start(bf16[32,2,1024]{2,1,0:T(2,128)(2,1)} %reshape.162), calls=%async_computation.2 | async-start | bytes 262144 | tf_op jit(solution)/shard_map/all_to_all | solution.py:195
  119.6 14.4 %all-gather = bf16[1,128,2048]{2,1,0:T(8,128)(2,1)S(1)} all-gather(bf16[1,128,1024]{2,1,0:T(8,128)(2,1)S(1)} %copy-done.7), channel_id=2, replica_groups=mesh['dp'=8,'ctx'=32,'tp'=2] {'tp'}, dimensions={2}, use_global_device_ids=true | all-gather | bytes 786432 | tf_op jit(solution)/shard_map/all_gather | solution.py:204
  134.1 48.3 %all-gather.3.cloned.1.call-done = bf16[2048,512]{1,0:T(8,128)(2,1)} async-done(((bf16[64,512]{1,0:T(8,128)(2,1)}), bf16[2048,512]{1,0:T(8,128)(2,1)}) %all-gather.3.cloned.1.call-update) | async-done | bytes 2097168 | tf_op jit(solution)/shard_map/all_gather | solution.py:197
  182.3 2.7 convolution_convert_fusion.2
  187.1 7.9 all-to-all-start.3
  195.6 1.8 fusion.46
  197.4 2.5 copy.68
  200.0 9.7 all-to-all-done.3
  212.6 53.6 %while.97 = (s32[]{:T(128)}, f32[4096,128]{0,1:T(8,128)S(1)}, bf16[2,512,64]{1,2,0:T(8,128)(2,1)}, s32[2,512]{1,0:T(2,128)S(1)}, bf16[2,512,64]{2,1,0:T(8,128)(2...) while((s32[]{:T(128)}, f32[4096,128]{0,1:T(8,128)S(1)}, ...), condition=%wide.region_17.18_spmd, body=%wide.region_13.17_spmd.sunk | while | flops 170394640 | bytes 7363270 | solution.py:236
  217.8 14.0 %while.100 = (s32[]{:T(128)}, f32[512,64]{0,1:T(8,128)S(1)}, f32[4096,128]{0,1:T(8,128)S(1)}, s32[]{:T(128)}, s32[512]{0:T(512)S(1)}, /*index=5*/bf16[4096,64]{1...) while((s32[]{:T(128)}, f32[512,64]{0,1:T(8,128)S(1)}, ...), condition=%wide.region_16.16_spmd, body=%wide.region_15.15_spmd.sunk | while | flops 170361344 | bytes 6760655 | solution.py:108
  217.8 1.3 fusion.104
  237.6 27.9 %while.100 = (s32[]{:T(128)}, f32[512,64]{0,1:T(8,128)S(1)}, f32[4096,128]{0,1:T(8,128)S(1)}, s32[]{:T(128)}, s32[512]{0:T(512)S(1)}, /*index=5*/bf16[4096,64]{1...) while((s32[]{:T(128)}, f32[512,64]{0,1:T(8,128)S(1)}, ...), condition=%wide.region_16.16_spmd, body=%wide.region_15.15_spmd.sunk | while | flops 170361344 | bytes 6760655 | solution.py:108
  237.6 1.3 fusion.104
  241.1 1.3 fusion.104
  244.6 1.3 fusion.104
  248.1 1.3 fusion.104
  251.6 1.3 fusion.104
  255.1 1.3 fusion.104
  258.6 1.3 fusion.104
  262.1 1.3 fusion.104
  266.2 1.8 copy.61
  268.0 1.7 select_convert_fusion
  269.7 2.2 collective-permute-start.2
  271.9 8.9 collective-permute-done.2
  280.7 1.9 convert_add_fusion
  283.4 3.6 collective-permute-start.3
  288.9 4.4 all-to-all-start.4
  293.6 1.8 fusion.49
  295.4 572.4 %reduce-scatter.7.cloned.1.call-done = bf16[64,512]{1,0:T(8,128)(2,1)} async-done(((bf16[2048,512]{1,0:T(8,128)(2,1)}), bf16[64,512]{1,0:T(8,128)(2,1)}) %reduce-scatter.7.cloned.1.call-update) | async-done | bytes 65552
  867.8 1.6 copy.69
  869.4 9.3 all-to-all-start.5
  878.8 1.6 convolution_convert_fusion.1
  881.7 13.5 %all-to-all-done.5 = bf16[32,32,128]{2,1,0:T(8,128)(2,1)S(1)} async-done(((bf16[32,32,128]{2,1,0:T(8,128)(2,1)}), bf16[32,32,128]{2,1,0:T(8,128)(2,1)S(1)}, u32[]{:S(2)}, u32[]{:S(2)}) %all-to-all-start.5) | async-done | bytes 262176 | tf_op jit(solution)/shard_map/all_to_all | solution.py:251
  897.5 54.4 %all-reduce.2.cloned.1.call-done = bf16[64,512]{0,1:T(8,128)(2,1)} async-done(((bf16[64,512]{0,1:T(8,128)(2,1)}), bf16[64,512]{0,1:T(8,128)(2,1)}) %all-reduce.2.cloned.1.call-update) | async-done | bytes 65552 | tf_op jit(solution)/shard_map/psum | solution.py:215
  951.9 1.6 copy.67
  953.5 27.1 %reduce-scatter.5.cloned.1.call-done = bf16[128,1024]{1,0:T(8,128)(2,1)} async-done(((bf16[128,2048]{1,0:T(8,128)(2,1)}), bf16[128,1024]{1,0:T(8,128)(2,1)}) %reduce-scatter.5.cloned.1.call-update) | async-done | bytes 262160 | tf_op jit(solution)/shard_map/reduce_scatter | solution.py:201
  (283 shorter events, 74.4 us)
Async XLA Ops:
  7.2 22.4 %copy-start.8 = (bf16[1,128,512]{2,1,0:T(8,128)(2,1)S(1)}, bf16[1,128,512]{2,1,0:T(8,128)(2,1)}, u32[]{:S(2)}) copy-start(bf16[1,128,512]{2,1,0:T(8,128)(2,1)} %param.16) | copy-start | bytes 393220
  7.2 23.5 %copy-start.9 = (s32[1,3,5]{2,0,1:T(1,128)S(1)}, s32[1,3,5]{2,0,1:T(1,128)}, u32[]{:S(2)}) copy-start(s32[1,3,5]{2,0,1:T(1,128)} %param.21) | copy-start | bytes 184
  10.3 39.2 %all-to-all-start.1 = ((bf16[32,32,128]{2,1,0:T(8,128)(2,1)}), bf16[32,32,128]{2,1,0:T(8,128)(2,1)S(1)}, u32[]{:S(2)}, u32[]{:S(2)}) async-start(bf16[32,32,128]{2,1,0:T(8,128)(2,1)} %bitcast.21), calls=%async_computation.1 | async-start | bytes 524288 | tf_op jit(solution)/shard_map/all_to_all | solution.py:150
  28.8 153.5 %all-gather.3.cloned.1.call-start = ((), (), s32[]{:S(2)}) async-start(), calls=%async_computation.8 | async-start | bytes 2162688 | tf_op jit(solution)/shard_map/all_gather | solution.py:197
  49.6 20.2 %all-to-all-start = ((bf16[32,2,1024]{2,1,0:T(2,128)(2,1)}), bf16[32,2,1024]{2,1,0:T(2,128)(2,1)S(1)}, u32[]{:S(2)}, u32[]{:S(2)}) async-start(bf16[32,2,1024]{2,1,0:T(2,128)(2,1)} %reshape.160), calls=%async_computation | async-start | bytes 262144 | tf_op jit(solution)/shard_map/all_to_all | solution.py:149
  54.8 10.3 %collective-permute-start = (bf16[1,32,32,128]{3,2,0,1:T(8,128)(2,1)S(1)}, bf16[1,32,32,128]{3,2,0,1:T(8,128)(2,1)S(1)}, u32[]{:S(2)}, u32[]{:S(2)}) collective-permute-start(bf16[1,32,32,128]{3,2,0,1:T(8,128)(2,1)S(1)} %bitcast.178), channel_id=1, source_target_pairs={{0,2},{2,0},{4,6},{6,4},{8,10},{10,8},{12,14},{14,12},{16,18},{18,... | collective-permute-start | bytes 786440 | tf_op jit(solution)/shard_map/ppermute | solution.py:13
  65.1 14.1 %collective-permute-start.1 = (bf16[2,32,32,128]{3,2,0,1:T(8,128)(2,1)S(1)}, bf16[2,32,32,128]{3,2,0,1:T(8,128)(2,1)S(1)}, u32[]{:S(2)}, u32[]{:S(2)}) collective-permute-start(bf16[2,32,32,128]{3,2,0,1:T(8,128)(2,1)S(1)} %maximum_select_fusion.1), channel_id=1, source_target_pairs={{0,4},{2,6},{4,0},{6,2},{8,12},{10,14},{12,8},{14,10},{16,20},{18,... | collective-permute-start | bytes 1572872 | tf_op jit(solution)/shard_map/ppermute | solution.py:13
  79.7 39.9 %copy-start.7 = (bf16[1,128,1024]{2,1,0:T(8,128)(2,1)S(1)}, bf16[1,128,1024]{2,1,0:T(8,128)(2,1)}, u32[]{:S(2)}) copy-start(bf16[1,128,1024]{2,1,0:T(8,128)(2,1)} %param.20) | copy-start | bytes 786436
  104.6 80.5 %copy-start = (bf16[4096,64]{1,0:T(8,128)(2,1)}, bf16[4096,64]{1,0:T(8,128)(2,1)S(1)}, u32[]{:S(2)}) copy-start(bf16[4096,64]{1,0:T(8,128)(2,1)S(1)} %get-tuple-element.1096) | copy-start | bytes 1572868
  104.6 80.5 %copy-start.1 = (bf16[2,512,64]{2,1,0:T(8,128)(2,1)}, bf16[2,512,64]{2,1,0:T(8,128)(2,1)S(1)}, u32[]{:S(2)}) copy-start(bf16[2,512,64]{2,1,0:T(8,128)(2,1)S(1)} %get-tuple-element.1098) | copy-start | bytes 393220
  105.6 81.4 %all-to-all-start.2 = ((bf16[32,2,1024]{2,1,0:T(2,128)(2,1)}), bf16[32,2,1024]{2,1,0:T(2,128)(2,1)S(1)}, u32[]{:S(2)}, u32[]{:S(2)}) async-start(bf16[32,2,1024]{2,1,0:T(2,128)(2,1)} %reshape.162), calls=%async_computation.2 | async-start | bytes 262144 | tf_op jit(solution)/shard_map/all_to_all | solution.py:195
  134.1 53.0 %copy-start.4 = (bf16[1,128,2048]{2,1,0:T(8,128)(2,1)}, bf16[1,128,2048]{2,1,0:T(8,128)(2,1)S(1)}, u32[]{:S(2)}) copy-start(bf16[1,128,2048]{2,1,0:T(8,128)(2,1)S(1)} %all-gather) | copy-start | bytes 1572868
  187.1 22.6 %all-to-all-start.3 = ((bf16[32,2,1024]{2,1,0:T(2,128)(2,1)}), bf16[32,2,1024]{2,1,0:T(2,128)(2,1)}, u32[]{:S(2)}, u32[]{:S(2)}) async-start(bf16[32,2,1024]{2,1,0:T(2,128)(2,1)} %reshape.164), calls=%async_computation.4 | async-start | bytes 262144 | tf_op jit(solution)/shard_map/all_to_all | solution.py:216
  194.9 672.8 %reduce-scatter.7.cloned.1.call-start = ((), (), s32[]{:S(2)}) async-start(), calls=%async_computation.11 | async-start | bytes 2162688
  195.6 4.3 copy-start.5
  210.8 0.9 copy-start.3
  269.7 11.0 %collective-permute-start.2 = (bf16[2,32,32,128]{3,2,0,1:T(8,128)(2,1)S(1)}, bf16[2,32,32,128]{3,2,0,1:T(8,128)(2,1)S(1)}, u32[]{:S(2)}, u32[]{:S(2)}) collective-permute-start(bf16[2,32,32,128]{3,2,0,1:T(8,128)(2,1)S(1)} %select_convert_fusion), channel_id=1, source_target_pairs={{0,4},{2,6},{4,0},{6,2},{8,12},{10,14},{12,8},{14,10},{16,20},{18,... | collective-permute-start | bytes 1572872 | tf_op jit(solution)/shard_map/ppermute | solution.py:13
  282.6 596.2 %copy-start.2 = (bf16[2048,512]{1,0:T(8,128)(2,1)S(1)}, bf16[2048,512]{1,0:T(8,128)(2,1)}, u32[]{:S(2)}) copy-start(bf16[2048,512]{1,0:T(8,128)(2,1)} %all-gather.3.cloned.1.call-done) | copy-start | bytes 6291460
  282.6 596.2 %copy-start.6 = (bf16[128,512]{1,0:T(8,128)(2,1)S(1)}, bf16[128,512]{1,0:T(8,128)(2,1)}, u32[]{:S(2)}) copy-start(bf16[128,512]{1,0:T(8,128)(2,1)} %copy-done.5) | copy-start | bytes 393220
  283.4 10.2 %collective-permute-start.3 = (bf16[1,32,32,128]{3,2,0,1:T(8,128)(2,1)}, bf16[1,32,32,128]{3,2,0,1:T(8,128)(2,1)}, u32[]{:S(2)}, u32[]{:S(2)}) collective-permute-start(bf16[1,32,32,128]{3,2,0,1:T(8,128)(2,1)} %select_convert_fusion.1), channel_id=1, source_target_pairs={{0,2},{2,0},{4,6},{6,4},{8,10},{10,8},{12,14},{14,12},{16,18},{18,... | collective-permute-start | bytes 786440 | tf_op jit(solution)/shard_map/ppermute | solution.py:13
  288.9 580.4 %all-to-all-start.4 = ((bf16[32,2,1024]{2,1,0:T(2,128)(2,1)}), bf16[32,2,1024]{2,1,0:T(2,128)(2,1)S(1)}, u32[]{:S(2)}, u32[]{:S(2)}) async-start(bf16[32,2,1024]{2,1,0:T(2,128)(2,1)} %reshape.166), calls=%async_computation.5 | async-start | bytes 262144 | tf_op jit(solution)/shard_map/all_to_all | solution.py:250
  293.4 658.5 %all-reduce.2.cloned.1.call-start = ((), (), s32[]{:S(2)}) async-start(), calls=%async_computation.10 | async-start | bytes 262144 | tf_op jit(solution)/shard_map/psum | solution.py:215
  869.4 25.9 %all-to-all-start.5 = ((bf16[32,32,128]{2,1,0:T(8,128)(2,1)}), bf16[32,32,128]{2,1,0:T(8,128)(2,1)S(1)}, u32[]{:S(2)}, u32[]{:S(2)}) async-start(bf16[32,32,128]{2,1,0:T(8,128)(2,1)} %fusion.49), calls=%async_computation.6 | async-start | bytes 524288 | tf_op jit(solution)/shard_map/all_to_all | solution.py:251
  878.7 101.9 %reduce-scatter.5.cloned.1.call-start = ((), (), s32[]{:S(2)}) async-start(), calls=%async_computation.9 | async-start | bytes 786432 | tf_op jit(solution)/shard_map/reduce_scatter | solution.py:201
Sparse Core Ops, SparseCore 0:
  32.8 149.5 all-gather.2
  200.2 667.5 reduce-scatter.6
  870.1 81.7 all-reduce.1
  955.3 25.2 reduce-scatter.4
where the time goes:
time: 989 us; the launch traced here: 987 us
  waiting for transfers between devices  770 us (78%)
  starting transfers between devices  72.9 us (7%)
  matrix products  57.8 us (6%)
  local copies, waits for them, and re-layouts  30.5 us (3%)
  other arithmetic  14.8 us (1%)
  blocking collectives  14.4 us (1%)
  between operations  14.3 us (1%)
  loops' own time  12.7 us (1%)
    unnamed x5, waiting for transfers between devices  573 us
    psum x1, waiting for transfers between devices, body(): grad_weight = lax.psum(weight_part, 'dp').astype(jnp.float32)  54.4 us
    all_gather x1, waiting for transfers between devices, body(): weight_full = lax.all_gather(out_weight, 'ctx', axis=0, tiled=True)  48.3 us
    reduce_scatter x1, waiting for transfers between devices, body(): lax.psum_scatter(partial_out.astype(jnp.bfloat16), 'tp', scatter_dimensio...  27.1 us
    ppermute x4, waiting for transfers between devices, from_partner(): lax.ppermute(shard, axis, [(i, i ^ 1 << bit) for i in range(lax.axis_size...  23.6 us
    dot_general x24, matrix products, tile_scores(): lax.dot_general(query_rows, tile_keys, (((1,), (1,)), ((), ())), preferre...  19.9 us
  transfers between devices with their start and end apart: 14, of which 11 were waited for; matrix products, arithmetic and copies ran while one was open for 10% of the time, Pallas kernels for 0%

commit v1 on v0

v1 whole, which is shorter than its diff:
```python
import functools

import jax
import jax.numpy as jnp
from jax import lax
from jax.experimental import pallas as pl
from jax.experimental.pallas import tpu as pltpu
from jax.sharding import PartitionSpec as P

MESH = pl.DeviceIdType.MESH
HS = 64
NEG_FILL = -1e30
TILE = 512
BF = jnp.bfloat16
F32 = jnp.float32
VMEM_LIMIT = 56 * 2**20


def swap_halves(first, second):
    low = lax.broadcasted_iota(jnp.int32, first.shape, 1) < HS
    first, second = first.astype(F32), second.astype(F32)
    return (
        jnp.where(low, first, pltpu.roll(second, HS, 1)).astype(BF),
        jnp.where(low, pltpu.roll(first, HS, 1), second).astype(BF),
    )


def remote(src, dst, send_sem, recv_sem, device):
    return pltpu.make_async_remote_copy(
        src_ref=src,
        dst_ref=dst,
        send_sem=send_sem,
        recv_sem=recv_sem,
        device_id=device,
        device_id_type=MESH,
    )


def places():
    ctx = lax.axis_index("ctx")
    dp = lax.axis_index("dp")
    tp = lax.axis_index("tp")
    return ctx, ctx // 4, ctx % 4, dp // 2, dp % 2, tp


def flip_x(member):
    return member + 1 - 2 * (member % 2)


def flip_z(member):
    return member + 2 - 4 * (member // 2)


def greet(devices):
    barrier = pltpu.get_barrier_semaphore()
    for device in devices:
        pl.semaphore_signal(barrier, inc=1, device_id=device, device_id_type=MESH)
    return lambda: pl.semaphore_wait(barrier, len(devices))


def gather_kernel(
    q_ref, k_ref, v_ref, w_ref, g_ref,
    qh_ref, kv_ref, gh_ref, wf_ref, gf_ref,
    kv_out, q_out, g_out,
    local_sem, kv_s, kv_r, q_s, q_r, w_s, w_r, gh_s, gh_r, m_s, m_r, y_s, y_r, one_s, one_r,
):
    ctx, spot, member, row, core, tp = places()
    peers = [{"ctx": ((spot + i) % 8) * 4 + member} for i in range(1, 8)]
    sources = [(spot + 8 - i) % 8 for i in range(1, 8)]
    x_dev = {"ctx": spot * 4 + flip_x(member)}
    z_dev = {"ctx": spot * 4 + flip_z(member)}
    y_devs = [{"dp": ((row + i) % 4) * 2 + core} for i in range(1, 4)]
    core_dev = {"dp": row * 2 + 1 - core}
    tp_dev = {"tp": 1 - tp}
    ready = greet(peers + [x_dev, z_dev] + y_devs + [core_dev, tp_dev])

    w_rows = pl.ds(pl.multiple_of(core * 32, 32), 32)
    w_cols = pl.ds(pl.multiple_of(row * 128, 128), 128)
    w_piece = w_ref.at[w_rows, w_cols]
    own_w = pltpu.make_async_copy(w_piece, wf_ref.at[spot, member, w_rows, w_cols], local_sem.at[0])
    own_g = pltpu.make_async_copy(g_ref, gf_ref.at[tp], local_sem.at[1])
    own_w.start()
    own_g.start()
    for pair in range(4):
        cols = slice(pair * 128, (pair + 1) * 128)
        even, odd = swap_halves(k_ref[:, cols], v_ref[:, cols])
        kv_out[2 * pair] = even
        kv_out[2 * pair + 1] = odd
        even, odd = swap_halves(q_ref[:64, cols], q_ref[64:, cols])
        q_out[2 * pair] = even
        q_out[2 * pair + 1] = odd
    own_kv = pltpu.make_async_copy(kv_out.at[spot], kv_ref.at[spot, member], local_sem.at[2])
    own_q = pltpu.make_async_copy(q_out.at[spot], qh_ref.at[spot], local_sem.at[3])
    own_kv.start()
    own_q.start()
    ready()

    sent = []

    def send(*copy_args):
        copy = remote(*copy_args)
        copy.start()
        sent.append(copy)

    def got(dst, recv_sem):
        remote(dst, dst, one_s.at[0], recv_sem, core_dev).wait_recv()

    for i in range(7):
        send(w_piece, wf_ref.at[spot, member, w_rows, w_cols], w_s.at[i], w_r.at[i], peers[i])
    send(g_ref, gf_ref.at[tp], one_s.at[0], one_r.at[0], tp_dev)
    for i in range(7):
        send(kv_out.at[(spot + i + 1) % 8], kv_ref.at[spot, member], kv_s.at[i], kv_r.at[i], peers[i])
    for i in range(7):
        send(q_out.at[(spot + i + 1) % 8], qh_ref.at[spot], q_s.at[i], q_r.at[i], peers[i])

    def w_slab(which):
        return wf_ref.at[:, which, w_rows, w_cols]

    def kv_slab(which):
        return kv_ref.at[:, which]

    own_w.wait()
    for i in range(7):
        got(wf_ref.at[sources[i], member, w_rows, w_cols], w_r.at[i])
    send(w_slab(member), w_slab(member), m_s.at[0], m_r.at[0], x_dev)
    send(w_slab(member), w_slab(member), m_s.at[1], m_r.at[1], z_dev)
    own_kv.wait()
    for i in range(7):
        got(kv_ref.at[sources[i], member], kv_r.at[i])
    send(kv_slab(member), kv_slab(member), m_s.at[3], m_r.at[3], x_dev)
    send(kv_slab(member), kv_slab(member), m_s.at[4], m_r.at[4], z_dev)
    got(w_slab(flip_x(member)), m_r.at[0])
    send(w_slab(flip_x(member)), w_slab(flip_x(member)), m_s.at[2], m_r.at[2], z_dev)
    got(w_slab(flip_z(member)), m_r.at[1])
    got(w_slab(flip_z(flip_x(member))), m_r.at[2])
    w_part = wf_ref.at[:, :, w_rows, w_cols]
    for i in range(3):
        send(w_part, w_part, y_s.at[i], y_r.at[i], y_devs[i])
    got(kv_slab(flip_x(member)), m_r.at[3])
    send(kv_slab(flip_x(member)), kv_slab(flip_x(member)), m_s.at[5], m_r.at[5], z_dev)
    for i in range(3):
        from_row = (row + 3 - i) % 4
        got(wf_ref.at[:, :, w_rows, pl.ds(pl.multiple_of(from_row * 128, 128), 128)], y_r.at[i])
    w_half = wf_ref.at[:, :, w_rows, :]
    send(w_half, w_half, one_s.at[1], one_r.at[1], core_dev)
    own_g.wait()
    got(gf_ref.at[1 - tp], one_r.at[0])
    got(wf_ref.at[:, :, pl.ds(pl.multiple_of(32 - core * 32, 32), 32), :], one_r.at[1])

    weight = wf_ref[...].reshape(2048, 512)
    grad_attn = jnp.dot(gf_ref[0], weight[:1024], preferred_element_type=F32)
    grad_attn += jnp.dot(gf_ref[1], weight[1024:], preferred_element_type=F32)
    grad_attn = grad_attn.astype(BF)
    for pair in range(4):
        cols = slice(pair * 128, (pair + 1) * 128)
        even, odd = swap_halves(grad_attn[:64, cols], grad_attn[64:, cols])
        g_out[2 * pair] = even
        g_out[2 * pair + 1] = odd
    own_gh = pltpu.make_async_copy(g_out.at[spot], gh_ref.at[spot], local_sem.at[4])
    own_gh.start()
    for i in range(7):
        send(g_out.at[(spot + i + 1) % 8], gh_ref.at[spot], gh_s.at[i], gh_r.at[i], peers[i])
    own_q.wait()
    own_gh.wait()
    for i in range(7):
        got(qh_ref.at[sources[i]], q_r.at[i])
    got(kv_slab(flip_z(member)), m_r.at[4])
    got(kv_slab(flip_z(flip_x(member))), m_r.at[5])
    for i in range(7):
        got(gh_ref.at[sources[i]], gh_r.at[i])
    for copy in sent:
        copy.wait_send()


def attention_kernel(seg_ref, q_ref, g_ref, kv_ref, ap_ref, dq_ref, dkv_ref, s_ref, dp_ref, p_ref, acc_ref):
    member = lax.axis_index("ctx") % 4
    low = lax.broadcasted_iota(jnp.int32, (64, 128), 1) < HS
    acc_ref[...] = jnp.zeros_like(acc_ref)

    def reach_of(position):
        reach = position
        for seg in range(5):
            start, length, flag = seg_ref[0, seg], seg_ref[1, seg], seg_ref[2, seg]
            inside = (position >= start) & (position < start + length) & (flag == 1)
            reach = jnp.where(inside, start + length - 1, reach)
        return reach

    def fold(tile, op):
        parts = [tile[:, c * 128:(c + 1) * 128] for c in range(TILE // 128)]
        while len(parts) > 1:
            parts = [op(parts[c], parts[c + 1]) for c in range(0, len(parts), 2)]
        return parts[0]

    def block(index, carry):
        begin = (4 * index + member) * 128
        qp = q_ref[index].astype(F32) * HS ** -0.5
        gp = g_ref[index].astype(F32)
        query = jnp.concatenate(
            [jnp.where(low, qp, 0.0), jnp.where(low, pltpu.roll(qp, HS, 1), 0.0)], axis=0
        )
        grad = jnp.concatenate(
            [jnp.where(low, 0.0, pltpu.roll(gp, HS, 1)), jnp.where(low, 0.0, gp)], axis=0
        )
        both = jnp.concatenate([query.astype(BF), grad.astype(BF)], axis=0)
        reach = reach_of(begin + lax.broadcasted_iota(jnp.int32, (128, 1), 0))
        tiles = reach_of(begin + 127) // TILE + 1

        def score(t, top):
            keys = pl.ds(pl.multiple_of(t * TILE, TILE), TILE)
            product = lax.dot_general(
                both, kv_ref[keys, :], (((1,), (1,)), ((), ())), preferred_element_type=F32
            )
            offset = t * TILE + lax.broadcasted_iota(jnp.int32, (128, TILE), 1)
            scores = jnp.where(offset <= reach, product[:128], NEG_FILL)
            s_ref[:, keys] = scores
            dp_ref[:, keys] = product[128:]
            return jnp.maximum(top, fold(scores, jnp.maximum))

        top = lax.fori_loop(0, tiles, score, jnp.full((128, 128), NEG_FILL, F32))
        top = jnp.max(top, axis=1, keepdims=True)

        def mix(t, carry):
            total, out = carry
            keys = pl.ds(pl.multiple_of(t * TILE, TILE), TILE)
            probs = jnp.exp(s_ref[:, keys] - top)
            probs_low = probs.astype(BF)
            p_ref[:, keys] = probs_low
            out = out + jnp.dot(probs_low, kv_ref[keys, :], preferred_element_type=F32)
            return total + fold(probs, jnp.add), out

        zeros = jnp.zeros((128, 128), F32)
        total, out = lax.fori_loop(0, tiles, mix, (zeros, zeros))
        inverse = 1.0 / jnp.sum(total, axis=1, keepdims=True)
        out = (out * inverse).astype(BF).astype(F32)
        delta = jnp.sum(grad * out, axis=1, keepdims=True)
        ap_ref[index] = jnp.where(low, pltpu.roll(out[:64], HS, 1), out[64:]).astype(BF)
        rows = jnp.concatenate([(query * inverse).astype(BF), (grad * inverse).astype(BF)], axis=0)

        def back(t, grad_query):
            keys = pl.ds(pl.multiple_of(t * TILE, TILE), TILE)
            probs_low = p_ref[:, keys]
            grad_scores = (probs_low.astype(F32) * (dp_ref[:, keys] - delta)).astype(BF)
            stacked = jnp.concatenate([grad_scores, probs_low], axis=0)
            acc_ref[keys, :] += lax.dot_general(
                stacked, rows, (((0,), (0,)), ((), ())), preferred_element_type=F32
            )
            return grad_query + jnp.dot(grad_scores, kv_ref[keys, :], preferred_element_type=F32)

        grad_query = lax.fori_loop(0, tiles, back, zeros) * (inverse * HS ** -0.5)
        dq_ref[index] = jnp.where(low, grad_query[:64], pltpu.roll(grad_query[64:], HS, 1)).astype(BF)
        return carry

    lax.fori_loop(0, 8, block, 0)
    dkv_ref[...] = acc_ref[...].astype(BF)


def return_kernel(
    ap_ref, dq_ref, dkv_ref, wf_ref, gf_ref,
    out_ref, gq_ref, gk_ref, gv_ref, gw_ref,
    a_in, dq_in, kv_in, z_in, z_sum, x_in, kv_sum, tp_out, tp_in,
    wp, core_in, core_sum, y_in, y_sum, m_in, m_sum, s_in, piece,
    local_sem, a_s, a_r, dq_s, dq_r, kv_s, kv_r, z_s, z_r, x_s, x_r,
    y_s, y_r, m_s, m_r, s_s, s_r, d_s, d_r, one_s, one_r,
):
    ctx, spot, member, row, core, tp = places()
    peers = [{"ctx": ((spot + i) % 8) * 4 + member} for i in range(1, 8)]
    sources = [(spot + 8 - i) % 8 for i in range(1, 8)]
    group = [{"ctx": spot * 4 + (member + i) % 4} for i in range(1, 4)]
    x_dev = {"ctx": spot * 4 + flip_x(member)}
    z_dev = {"ctx": spot * 4 + flip_z(member)}
    dp = row * 2 + core
    dp_devs = [{"dp": (dp + i) % 8} for i in range(1, 8)]
    y_devs = [{"dp": ((row + i) % 4) * 2 + core} for i in range(1, 4)]
    core_dev = {"dp": row * 2 + 1 - core}
    tp_dev = {"tp": 1 - tp}
    ready = greet(peers + group + dp_devs + [tp_dev])
    ready()

    sent = []

    def send(*copy_args):
        copy = remote(*copy_args)
        copy.start()
        sent.append(copy)

    def got(dst, recv_sem):
        remote(dst, dst, one_s.at[0], recv_sem, core_dev).wait_recv()

    z_bit, x_bit = member // 2, member % 2
    own_a = pltpu.make_async_copy(ap_ref.at[spot], a_in.at[spot], local_sem.at[0])
    own_dq = pltpu.make_async_copy(dq_ref.at[spot], dq_in.at[spot], local_sem.at[1])
    own_a.start()
    own_dq.start()
    for i in range(7):
        send(ap_ref.at[(spot + i + 1) % 8], a_in.at[spot], a_s.at[i], a_r.at[i], peers[i])
    for half in range(2):
        blocks = pl.ds(half * 4, 4)
        send(dkv_ref.at[blocks, pl.ds(2 - 2 * z_bit, 2)], z_in.at[blocks], z_s.at[half], z_r.at[half], z_dev)
    for i in range(7):
        send(dq_ref.at[(spot + i + 1) % 8], dq_in.at[spot], dq_s.at[i], dq_r.at[i], peers[i])

    own_a.wait()
    for i in range(7):
        got(a_in.at[sources[i]], a_r.at[i])
    tops, bottoms = [], []
    for pair in range(4):
        top, bottom = swap_halves(a_in[2 * pair], a_in[2 * pair + 1])
        tops.append(top)
        bottoms.append(bottom)
    attn = jnp.concatenate(
        [jnp.concatenate(tops, axis=1), jnp.concatenate(bottoms, axis=1)], axis=0
    )
    for half in range(2):
        part = lax.dot_general(
            gf_ref[half], attn, (((0,), (0,)), ((), ())), preferred_element_type=F32
        )
        wp[pl.ds(half * 4, 4)] = part.astype(BF).reshape(4, 4, 2, 32, 512)
    send(wp.at[:, :, 1 - core], core_in, one_s.at[1], one_r.at[1], core_dev)

    weight = wf_ref[...].reshape(2, 1024, 512)
    for half in range(2):
        part = lax.dot_general(
            attn, weight[half], (((1,), (1,)), ((), ())), preferred_element_type=F32
        )
        tp_out[half] = part.astype(BF)
    send(tp_out.at[1 - tp], tp_in, one_s.at[0], one_r.at[0], tp_dev)

    for half in range(2):
        blocks = pl.ds(half * 4, 4)
        got(z_in.at[blocks], z_r.at[half])
        z_sum[blocks] = (
            dkv_ref[blocks, pl.ds(2 * z_bit, 2)].astype(F32) + z_in[blocks].astype(F32)
        ).astype(BF)
        send(z_sum.at[blocks, 1 - x_bit], x_in.at[blocks], x_s.at[half], x_r.at[half], x_dev)

    got(core_in, one_r.at[1])
    core_sum[...] = (wp[:, :, core].astype(F32) + core_in[...].astype(F32)).astype(BF)
    for i in range(3):
        to_row = (row + i + 1) % 4
        cols = pl.ds(pl.multiple_of(to_row * 128, 128), 128)
        send(core_sum.at[:, :, :, cols], y_in.at[i], y_s.at[i], y_r.at[i], y_devs[i])

    for half in range(2):
        blocks = pl.ds(half * 4, 4)
        got(x_in.at[blocks], x_r.at[half])
        kv_sum[blocks] = (z_sum[blocks, x_bit].astype(F32) + x_in[blocks].astype(F32)).astype(BF)
    own_kv = pltpu.make_async_copy(kv_sum.at[spot], kv_in.at[spot], local_sem.at[2])
    own_kv.start()
    for i in range(7):
        send(kv_sum.at[(spot + i + 1) % 8], kv_in.at[spot], kv_s.at[i], kv_r.at[i], peers[i])

    got(tp_in, one_r.at[0])
    out_ref[...] = (tp_out[tp].astype(F32) + tp_in[...].astype(F32)).astype(BF)

    for i in range(3):
        got(y_in.at[i], y_r.at[i])
    cols = pl.ds(pl.multiple_of(row * 128, 128), 128)
    y_sum[...] = (
        (core_sum[:, :, :, cols].astype(F32) + y_in[0].astype(F32))
        + (y_in[1].astype(F32) + y_in[2].astype(F32))
    ).astype(BF)
    for i in range(3):
        send(y_sum.at[:, (member + i + 1) % 4], m_in.at[i], m_s.at[i], m_r.at[i], group[i])

    own_dq.wait()
    for i in range(7):
        got(dq_in.at[sources[i]], dq_r.at[i])
    for pair in range(4):
        cols = slice(pair * 128, (pair + 1) * 128)
        top, bottom = swap_halves(dq_in[2 * pair], dq_in[2 * pair + 1])
        gq_ref[:64, cols] = top
        gq_ref[64:, cols] = bottom

    for i in range(3):
        got(m_in.at[i], m_r.at[i])
    m_sum[...] = (
        (y_sum[:, member].astype(F32) + m_in[0].astype(F32))
        + (m_in[1].astype(F32) + m_in[2].astype(F32))
    ).astype(BF)
    for i in range(7):
        send(m_sum.at[(spot + i + 1) % 8], s_in.at[i], s_s.at[i], s_r.at[i], peers[i])

    own_kv.wait()
    for i in range(7):
        got(kv_in.at[sources[i]], kv_r.at[i])
    for pair in range(4):
        cols = slice(pair * 128, (pair + 1) * 128)
        keys, values = swap_halves(kv_in[2 * pair], kv_in[2 * pair + 1])
        gk_ref[:, cols] = keys
        gv_ref[:, cols] = values

    total = m_sum[spot].astype(F32)
    for i in range(7):
        got(s_in.at[i], s_r.at[i])
        total = total + s_in[i].astype(F32)
    piece[...] = total
    spot_w = gw_ref.at[
        pl.ds(pl.multiple_of(core * 32, 32), 32), pl.ds(pl.multiple_of(row * 128, 128), 128)
    ]
    own_w = pltpu.make_async_copy(piece, spot_w, local_sem.at[3])
    own_w.start()
    for i in range(7):
        send(piece, spot_w, d_s.at[i], d_r.at[i], dp_devs[i])
    own_w.wait()
    for i in range(7):
        source = (dp + 7 - i) % 8
        got(
            gw_ref.at[
                pl.ds(pl.multiple_of((source % 2) * 32, 32), 32),
                pl.ds(pl.multiple_of((source // 2) * 128, 128), 128),
            ],
            d_r.at[i],
        )
    for copy in sent:
        copy.wait_send()


def like(shape, dtype=BF):
    return jax.ShapeDtypeStruct(shape, dtype)


def dma(count):
    return pltpu.SemaphoreType.DMA((count,))


def body(query_states, key_states, value_states, out_weight, grad_output, segment_table):
    vmem = pl.BlockSpec(memory_space=pltpu.VMEM)
    smem = pl.BlockSpec(memory_space=pltpu.SMEM)
    scratch = lambda *shape: pltpu.VMEM(shape, BF)
    qh, kv, gh, wf, gf = pl.pallas_call(
        gather_kernel,
        out_shape=(
            like((8, 64, 128)),
            like((8, 4, 128, 128)),
            like((8, 64, 128)),
            like((8, 4, 64, 512)),
            like((2, 128, 1024)),
        ),
        in_specs=[vmem] * 5,
        out_specs=(vmem,) * 5,
        scratch_shapes=[
            scratch(8, 128, 128),
            scratch(8, 64, 128),
            scratch(8, 64, 128),
            dma(5),
            *[dma(7)] * 8,
            *[dma(6)] * 2,
            *[dma(3)] * 2,
            *[dma(2)] * 2,
        ],
        compiler_params=pltpu.CompilerParams(
            collective_id=0, has_side_effects=True, vmem_limit_bytes=VMEM_LIMIT
        ),
        name="gather_heads",
    )(query_states[0], key_states[0], value_states[0], out_weight, grad_output[0])
    ap, dq, dkv = pl.pallas_call(
        attention_kernel,
        out_shape=(like((8, 64, 128)), like((8, 64, 128)), like((4096, 128))),
        in_specs=[smem] + [vmem] * 3,
        out_specs=(vmem,) * 3,
        scratch_shapes=[
            pltpu.VMEM((128, 4096), F32),
            pltpu.VMEM((128, 4096), F32),
            pltpu.VMEM((128, 4096), BF),
            pltpu.VMEM((4096, 128), F32),
        ],
        compiler_params=pltpu.CompilerParams(vmem_limit_bytes=VMEM_LIMIT),
        name="attention",
    )(segment_table[0], qh, gh, kv.reshape(4096, 128))
    outs = pl.pallas_call(
        return_kernel,
        out_shape=(
            like((128, 1024)),
            like((128, 512)),
            like((128, 512)),
            like((128, 512)),
            like((64, 512), F32),
        ),
        in_specs=[vmem] * 5,
        out_specs=(vmem,) * 5,
        scratch_shapes=[
            scratch(8, 64, 128),
            scratch(8, 64, 128),
            scratch(8, 128, 128),
            scratch(8, 2, 128, 128),
            scratch(8, 2, 128, 128),
            scratch(8, 128, 128),
            scratch(8, 128, 128),
            scratch(2, 128, 1024),
            scratch(128, 1024),
            scratch(8, 4, 2, 32, 512),
            scratch(8, 4, 32, 512),
            scratch(8, 4, 32, 512),
            scratch(3, 8, 4, 32, 128),
            scratch(8, 4, 32, 128),
            scratch(3, 8, 32, 128),
            scratch(8, 32, 128),
            scratch(7, 32, 128),
            pltpu.VMEM((32, 128), F32),
            dma(4),
            *[dma(7)] * 6,
            *[dma(2)] * 4,
            *[dma(3)] * 4,
            *[dma(7)] * 4,
            *[dma(2)] * 2,
        ],
        compiler_params=pltpu.CompilerParams(
            collective_id=1, has_side_effects=True, vmem_limit_bytes=VMEM_LIMIT
        ),
        name="return_tokens",
    )(ap, dq, dkv.reshape(8, 4, 128, 128), wf, gf)
    layer, grad_q, grad_k, grad_v, grad_w = outs
    return (layer[None], grad_q[None], grad_k[None], grad_v[None], grad_w)


def solution(mesh):
    placed = (
        P("dp", "ctx", "tp"),
        P("dp", "ctx", "tp"),
        P("dp", "ctx", "tp"),
        P("ctx", "tp"),
        P("dp", "ctx", "tp"),
        P("dp", None, None),
    )
    return jax.shard_map(
        body,
        mesh=mesh,
        in_specs=placed,
        out_specs=(
            P("dp", "ctx", "tp"),
            P("dp", "ctx", "tp"),
            P("dp", "ctx", "tp"),
            P("dp", "ctx", "tp"),
            P("ctx", "tp"),
        ),
        check_vma=False,
    )
```

time: 989 us -> 187 us (0.19)
  waiting for transfers between devices: 770 us -> 0 us
  Pallas kernels: 0 us -> 175 us
  starting transfers between devices: 72.9 us -> 0 us
  matrix products: 57.8 us -> 0 us
  local copies, waits for them, and re-layouts: 30.5 us -> 9.2 us
  other arithmetic: 14.8 us -> 0 us
  blocking collectives: 14.4 us -> 0 us
  between operations: 14.3 us -> 0.65 us
  loops' own time: 12.7 us -> 0 us
    unnamed x5 -> x0, waiting for transfers between devices: 573 us -> none
    pallas_call x0 -> x3, Pallas kernels: none -> 175 us  [the longest x1 73.7 us: body(): pl.pallas_call(gather_kernel, out_shape=(like((8, 64, 128)), like((8, 4,...]
    all_to_all x6 -> x0, starting transfers between devices: 59.3 us -> none  [the longest x1 18.5 us: body(): lax.all_to_all(to_heads(pair_local.reshape(tokens_here, heads_here * 2 *...]
    dot_general x87 -> x0, matrix products: 57.8 us -> none  [the longest x24 19.9 us: tile_scores(): lax.dot_general(query_rows, tile_keys, (((1,), (1,)), ((), ())), preferre...]
    psum x1 -> x0, waiting for transfers between devices: 54.4 us -> none  [body(): grad_weight = lax.psum(weight_part, 'dp').astype(jnp.float32)]
    all_gather x1 -> x0, waiting for transfers between devices: 48.3 us -> none  [body(): weight_full = lax.all_gather(out_weight, 'ctx', axis=0, tiled=True)]
    all_to_all x6 -> x0, waiting for transfers between devices: 43.2 us -> none  [the longest x1 18.9 us: body(): lax.all_to_all(to_heads(pair_local.reshape(tokens_here, heads_here * 2 *...]
    reduce_scatter x1 -> x0, waiting for transfers between devices: 27.1 us -> none  [body(): lax.psum_scatter(partial_out.astype(jnp.bfloat16), 'tp', scatter_dimensio...]
  transfers between devices with their start and end apart: 14 -> 0, of which waited for: 11 -> 0; matrix products, arithmetic and copies ran while one was open for 10% -> 0% of each run, Pallas kernels for 0% -> 0%
where the time goes in v1:
time: 187 us; the launch traced here: 185 us
  Pallas kernels  175 us (94%)
  local copies, waits for them, and re-layouts  9.2 us (5%)
    pallas_call x1, Pallas kernels, body(): pl.pallas_call(gather_kernel, out_shape=(like((8, 64, 128)), like((8, 4,...  73.7 us
    pallas_call x1, Pallas kernels, body(): pl.pallas_call(return_kernel, out_shape=(like((128, 1024)), like((128, 51...  66.6 us
    pallas_call x1, Pallas kernels, body(): pl.pallas_call(attention_kernel, out_shape=(like((8, 64, 128)), like((8,...  35.1 us
    unnamed x6, local copies, waits for them, and re-layouts  9.2 us

profile of v1, /device:TPU:1, one launch (start us, length us, event | category | flops | bytes accessed | tf_op | source)
XLA Modules:
  0.0 185.3 jit_solution(14815262994706324996)
XLA Ops:
  0.6 1.3 copy.13
  1.9 73.7 %gather_heads.1 = (bf16[8,64,128]{2,1,0:T(8,128)(2,1)}, bf16[8,4,128,128]{3,2,1,0:T(8,128)(2,1)}, bf16[8,64,128]{2,1,0:T(8,128)(2,1)}, bf16[8,4,64,512]{3,2,1,0:T(8,128)(2,1)}, bf16[2,128,1024]{2,1,0:T(8,128)(2,1)}) custom-call(bf16[128,512]{1,0:T(8,128)(2,1)} %bitcast.20, bf16[128,512]{1,0:T(8,128)(2,1)} %bitcast.21, bf16[128,512]{1,0:T(8,128)(2,1)} %bitcast.22, ...), custom_call_target="tpu_custom_call" | custom-call | tf_op jit(solution)/shard_map/gather_heads/pallas_call | solution.py:430
  75.6 35.1 %attention.1 = (bf16[8,64,128]{2,1,0:T(8,128)(2,1)}, bf16[8,64,128]{2,1,0:T(8,128)(2,1)}, bf16[4096,128]{1,0:T(8,128)(2,1)}) custom-call(s32[3,5]{1,0:T(4,128)} %bitcast.23, bf16[8,64,128]{2,1,0:T(8,128)(2,1)} %get-tuple-element.18.q_ref, bf16[8,64,128]{2,1,0:T(8,128)(2,1)} %get-tuple-element.19.g_ref, bf16[4096,128]{1,0:T(8,128)(2,1)} %bitcast.13), custom_call_target="tpu_custom_call" | custom-call | tf_op jit(solution)/shard_map/attention/pallas_call | solution.py:456
  110.7 66.6 %return_tokens.1 = (bf16[128,1024]{1,0:T(8,128)(2,1)}, bf16[128,512]{1,0:T(8,128)(2,1)}, bf16[128,512]{1,0:T(8,128)(2,1)}, bf16[128,512]{1,0:T(8,128)(2,1)}, f32[64,512]{1,0:T(8,128)}) custom-call(bf16[8,64,128]{2,1,0:T(8,128)(2,1)} %get-tuple-element.21.ap_ref, bf16[8,64,128]{2,1,0:T(8,128)(2,1)} %get-tuple-element.22.dq_ref, ...), custom_call_target="tpu_custom_call" | custom-call | tf_op jit(solution)/shard_map/return_tokens/pallas_call | solution.py:470
  177.3 1.7 copy.19
  179.0 1.6 copy.20
  180.6 1.6 copy.21
  182.1 1.6 copy.22
  183.7 1.6 copy.23

commit v2 on v0

v2 whole, which is shorter than its diff:
```python
import functools

import jax
import jax.numpy as jnp
from jax import lax
from jax.experimental import pallas as pl
from jax.experimental.pallas import tpu as pltpu
from jax.sharding import PartitionSpec as P

MESH = pl.DeviceIdType.MESH
HS = 64
NEG_FILL = -1e30
TILE = 512
CHUNK = 128
BF = jnp.bfloat16
F32 = jnp.float32
VMEM_LIMIT = 56 * 2**20
W_HALF_STEP = 3
W_DONE_STEP = 5
PROJECT_STEP = 2
CORE_STEP = 4


def swap_halves(first, second):
    low = lax.broadcasted_iota(jnp.int32, first.shape, 1) < HS
    first, second = first.astype(F32), second.astype(F32)
    return (
        jnp.where(low, first, pltpu.roll(second, HS, 1)).astype(BF),
        jnp.where(low, pltpu.roll(first, HS, 1), second).astype(BF),
    )


def remote(src, dst, send_sem, recv_sem, device):
    return pltpu.make_async_remote_copy(
        src_ref=src,
        dst_ref=dst,
        send_sem=send_sem,
        recv_sem=recv_sem,
        device_id=device,
        device_id_type=MESH,
    )


def places():
    ctx = lax.axis_index("ctx")
    dp = lax.axis_index("dp")
    tp = lax.axis_index("tp")
    return ctx, ctx // 4, ctx % 4, dp // 2, dp % 2, tp


def greet(devices):
    barrier = pltpu.get_barrier_semaphore()
    for device in devices:
        pl.semaphore_signal(barrier, inc=1, device_id=device, device_id_type=MESH)
    return lambda: pl.semaphore_wait(barrier, len(devices))


def order(step):
    half = (step + 1) // 2
    return (step % 2) * half + (1 - step % 2) * ((8 - half) % 8)


def sublayer_kernel(
    seg_ref, q_ref, k_ref, v_ref, w_ref, g_ref,
    layer_ref, dq_in, dkv_in, gw_ref,
    kv_out, q_out, qh, kv, wf, gf, g_out, gh,
    reach_ref, query, grad, both, probs, tops, top, total, out, base, delta, grad_q, acc,
    a_out, a_in, dq_out, part, part_in, part_sum,
    tp_out, tp_in, wp, core_in, core_sum, y_in, y_sum, m_in, m_sum, s_in, piece,
    local_sem, w_s, w_r, q_s, q_r, kv_s, kv_r, fwd_s, fwd_r, wm_s, wm_r, wy_s, wy_r, gh_s, gh_r,
    a_s, a_r, part_s, part_r, dkv_s, dkv_r, dq_s, dq_r, y_s, y_r, m_s, m_r, s_s, s_r, d_s, d_r, one_s, one_r,
):
    ctx, spot, member, row, core, tp = places()
    near_first = [1, 7, 2, 6, 3, 5, 4]
    peer_spots = [(spot + i) % 8 for i in near_first]
    source_spots = [(spot + 8 - i) % 8 for i in near_first]
    peers = [{"ctx": s * 4 + member} for s in peer_spots]
    group = [{"ctx": spot * 4 + (member + i) % 4} for i in range(1, 4)]
    dp = row * 2 + core
    dp_devs = [{"dp": (dp + i) % 8} for i in range(1, 8)]
    y_devs = [{"dp": ((row + i) % 4) * 2 + core} for i in range(1, 4)]
    core_dev = {"dp": row * 2 + 1 - core}
    tp_dev = {"tp": 1 - tp}
    ready = greet(peers + group + dp_devs + [tp_dev])

    sent = []

    def send(*copy_args):
        copy = remote(*copy_args)
        copy.start()
        sent.append(copy)

    def got(dst, recv_sem):
        remote(dst, dst, one_s.at[0], recv_sem, core_dev).wait_recv()

    low = lax.broadcasted_iota(jnp.int32, (64, 128), 1) < HS

    w_rows = pl.ds(pl.multiple_of(core * 32, 32), 32)
    w_cols = pl.ds(pl.multiple_of(row * 128, 128), 128)
    w_piece = w_ref.at[w_rows, w_cols]
    own_w = pltpu.make_async_copy(w_piece, wf.at[spot, member, w_rows, w_cols], local_sem.at[0])
    own_g = pltpu.make_async_copy(g_ref, gf.at[tp], local_sem.at[1])
    own_w.start()
    own_g.start()
    for pair in range(4):
        cols = slice(pair * 128, (pair + 1) * 128)
        even, odd = swap_halves(k_ref[:, cols], v_ref[:, cols])
        kv_out[2 * pair] = even
        kv_out[2 * pair + 1] = odd
        even, odd = swap_halves(q_ref[:64, cols], q_ref[64:, cols])
        q_out[2 * pair] = even
        q_out[2 * pair + 1] = odd
    own_kv = pltpu.make_async_copy(kv_out.at[spot], kv.at[spot, member], local_sem.at[2])
    own_q = pltpu.make_async_copy(q_out.at[spot], qh.at[spot], local_sem.at[3])
    own_kv.start()
    own_q.start()
    ready()

    for i in range(7):
        send(w_piece, wf.at[spot, member, w_rows, w_cols], w_s.at[i], w_r.at[i], peers[i])
    for i in range(7):
        send(q_out.at[peer_spots[i]], qh.at[spot], q_s.at[i], q_r.at[i], peers[i])
    for i in range(7):
        send(kv_out.at[peer_spots[i]], kv.at[spot, member], kv_s.at[i], kv_r.at[spot], peers[i])
    send(g_ref, gf.at[tp], one_s.at[0], one_r.at[0], tp_dev)

    def forward_copies(t):
        return [
            remote(kv.at[t, member], kv.at[t, member], fwd_s.at[t * 3 + i], fwd_r.at[t * 3 + i], group[i])
            for i in range(3)
        ]

    own_kv.wait()
    for copy in forward_copies(spot):
        copy.start()

    def reach_of(position):
        reach = position
        for seg in range(5):
            start, length, flag = seg_ref[0, seg], seg_ref[1, seg], seg_ref[2, seg]
            inside = (position >= start) & (position < start + length) & (flag == 1)
            reach = jnp.where(inside, start + length - 1, reach)
        return reach

    for index in range(8):
        position = (4 * index + member) * 128 + lax.broadcasted_iota(jnp.int32, (128, 128), 0)
        reach_ref[index * 128:(index + 1) * 128, :] = reach_of(position) - lax.broadcasted_iota(
            jnp.int32, (128, 128), 1
        )
    top[...] = jnp.full_like(top, NEG_FILL)
    total[...] = jnp.zeros_like(total)
    out[...] = jnp.zeros_like(out)
    grad_q[...] = jnp.zeros_like(grad_q)

    own_w.wait()
    for i in range(7):
        got(wf.at[source_spots[i], member, w_rows, w_cols], w_r.at[i])
    w_slab = wf.at[:, member, w_rows, w_cols]
    for i in range(3):
        send(w_slab, w_slab, wm_s.at[i], wm_r.at[i], group[i])

    own_q.wait()
    for i in range(7):
        got(qh.at[source_spots[i]], q_r.at[i])
    for index in range(8):
        packed = qh[index].astype(F32) * HS ** -0.5
        query[index * 128:index * 128 + 64, :] = jnp.where(low, packed, 0.0).astype(BF)
        query[index * 128 + 64:(index + 1) * 128, :] = jnp.where(
            low, pltpu.roll(packed, HS, 1), 0.0
        ).astype(BF)

    def first_pair(t):
        return jnp.maximum(4 * t - 5 - member, 0) // 8

    def forward_tile(t):
        tile = kv[t].reshape(TILE, 128)

        def pair(index, carry):
            rows = pl.ds(pl.multiple_of(index * 256, 256), 256)
            scores = lax.dot_general(
                query[rows, :], tile, (((1,), (1,)), ((), ())), preferred_element_type=F32
            )
            reach = reach_ref[rows, :] - t * TILE
            parts = [
                jnp.where(reach >= c * CHUNK, scores[:, c * CHUNK:(c + 1) * CHUNK], NEG_FILL)
                for c in range(TILE // CHUNK)
            ]
            best = jnp.maximum(jnp.maximum(parts[0], parts[1]), jnp.maximum(parts[2], parts[3]))
            before = top[rows, :]
            now = jnp.maximum(before, jnp.max(best, axis=1, keepdims=True))
            shrink = jnp.exp(before - now)
            parts = [jnp.exp(p - now) for p in parts]
            total[rows, :] = total[rows, :] * shrink + ((parts[0] + parts[1]) + (parts[2] + parts[3]))
            low_probs = jnp.concatenate([p.astype(BF) for p in parts], axis=1)
            probs[t, rows, :] = low_probs
            out[rows, :] = out[rows, :] * shrink + jnp.dot(
                low_probs, tile, preferred_element_type=F32
            )
            top[rows, :] = now
            tops[t, rows, :] = now
            return carry

        lax.fori_loop(first_pair(t), 4, pair, 0)

    w_part = wf.at[:, :, w_rows, w_cols]
    w_half = wf.at[:, :, w_rows, :]

    def weight_copies():
        return [remote(w_part, w_part, wy_s.at[i], wy_r.at[i], y_devs[i]) for i in range(3)]

    def half_copy():
        return remote(w_half, w_half, one_s.at[1], one_r.at[1], core_dev)

    def grad_copies():
        return [
            remote(g_out.at[peer_spots[i]], gh.at[spot], gh_s.at[i], gh_r.at[i], peers[i])
            for i in range(7)
        ]

    own_gh = pltpu.make_async_copy(g_out.at[spot], gh.at[spot], local_sem.at[4])

    def forward_step(step, carry):
        t = (spot + order(step)) % 8

        @pl.when(step < 7)
        def _():
            later = (spot + order(step + 1)) % 8
            got(kv.at[later, member], kv_r.at[later])
            for copy in forward_copies(later):
                copy.start()

        for i in range(3):
            got(kv.at[t, (member + 3 - i) % 4], fwd_r.at[t * 3 + i])
        forward_tile(t)

        @pl.when(step == 0)
        def _():
            for i in range(3):
                got(wf.at[:, (member + 3 - i) % 4, w_rows, w_cols], wm_r.at[i])
            for copy in weight_copies():
                copy.start()

        @pl.when(step == W_HALF_STEP)
        def _():
            for i in range(3):
                from_row = (row + 3 - i) % 4
                got(wf.at[:, :, w_rows, pl.ds(pl.multiple_of(from_row * 128, 128), 128)], wy_r.at[i])
            half_copy().start()

        @pl.when(step == W_DONE_STEP)
        def _():
            got(wf.at[:, :, pl.ds(pl.multiple_of(32 - core * 32, 32), 32), :], one_r.at[1])
            own_g.wait()
            got(gf.at[1 - tp], one_r.at[0])
            weight = wf[...].reshape(2048, 512)
            grad_attn = jnp.dot(gf[0], weight[:1024], preferred_element_type=F32)
            grad_attn += jnp.dot(gf[1], weight[1024:], preferred_element_type=F32)
            grad_attn = grad_attn.astype(BF)
            for two in range(4):
                cols = slice(two * 128, (two + 1) * 128)
                even, odd = swap_halves(grad_attn[:64, cols], grad_attn[64:, cols])
                g_out[2 * two] = even
                g_out[2 * two + 1] = odd
            own_gh.start()
            for copy in grad_copies():
                copy.start()

        return carry

    lax.fori_loop(0, 8, forward_step, 0)

    def finish(index, carry):
        rows = pl.ds(pl.multiple_of(index * 128, 128), 128)
        row_sum = jnp.sum(total[rows, :], axis=1, keepdims=True)
        values = (out[rows, :] * (1.0 / row_sum)).astype(BF).astype(F32)
        out[rows, :] = values
        base[rows, :] = top[rows, :] + jnp.log(row_sum)
        a_out[index] = jnp.where(low, pltpu.roll(values[:64], HS, 1), values[64:]).astype(BF)
        return carry

    lax.fori_loop(0, 8, finish, 0)
    own_a = pltpu.make_async_copy(a_out.at[spot], a_in.at[spot], local_sem.at[5])
    own_a.start()
    for i in range(7):
        send(a_out.at[peer_spots[i]], a_in.at[spot], a_s.at[i], a_r.at[i], peers[i])

    own_gh.wait()
    for i in range(7):
        got(gh.at[source_spots[i]], gh_r.at[i])

    def spread(index, carry):
        rows = pl.ds(pl.multiple_of(index * 128, 128), 128)
        packed = gh[index].astype(F32)
        values = jnp.concatenate(
            [jnp.where(low, 0.0, pltpu.roll(packed, HS, 1)), jnp.where(low, 0.0, packed)], axis=0
        )
        grad[rows, :] = values.astype(BF)
        both[rows, :] = query[rows, :].astype(F32) + values
        delta[rows, :] = jnp.broadcast_to(
            jnp.sum(values * out[rows, :], axis=1, keepdims=True), (128, 128)
        )
        return carry

    lax.fori_loop(0, 8, spread, 0)

    def backward_tile(t):
        tile = kv[t].reshape(TILE, 128)
        acc[...] = jnp.zeros_like(acc)

        def pair(index, carry):
            rows = pl.ds(pl.multiple_of(index * 256, 256), 256)
            factor = jnp.exp(tops[t, rows, :] - base[rows, :])
            turned = jnp.transpose(both[rows, :] * factor).astype(BF)
            grad_probs = lax.dot_general(
                grad[rows, :], tile, (((1,), (1,)), ((), ())), preferred_element_type=F32
            )
            low_probs = probs[t, rows, :]
            shift = delta[rows, :]
            grad_scores = jnp.concatenate(
                [
                    (
                        low_probs[:, c * CHUNK:(c + 1) * CHUNK].astype(F32)
                        * (grad_probs[:, c * CHUNK:(c + 1) * CHUNK] - shift)
                    ).astype(BF)
                    for c in range(TILE // CHUNK)
                ],
                axis=1,
            )
            acc[:HS, :] += jnp.dot(turned[:HS], grad_scores, preferred_element_type=F32)
            acc[HS:, :] += jnp.dot(turned[HS:], low_probs, preferred_element_type=F32)
            grad_q[rows, :] += factor * jnp.dot(grad_scores, tile, preferred_element_type=F32)
            return carry

        lax.fori_loop(first_pair(t), 4, pair, 0)
        part[t] = jnp.transpose(acc[...]).astype(BF).reshape(4, 128, 128)

    def part_copies(t):
        return [
            remote(part.at[t, (member + i + 1) % 4], part_in.at[t, i], part_s.at[t * 3 + i], part_r.at[t * 3 + i], group[i])
            for i in range(3)
        ]

    def home_copy(t):
        return remote(part_sum.at[t], dkv_in.at[spot], dkv_s.at[t], dkv_r.at[spot], {"ctx": t * 4 + member})

    own_dkv = pltpu.make_async_copy(part_sum.at[spot], dkv_in.at[spot], local_sem.at[6])

    def send_home(t):
        for i in range(3):
            got(part_in.at[t, i], part_r.at[t * 3 + i])
        part_sum[t] = (
            (part[t, member].astype(F32) + part_in[t, 0].astype(F32))
            + (part_in[t, 1].astype(F32) + part_in[t, 2].astype(F32))
        ).astype(BF)

    def core_copy():
        return remote(wp.at[:, :, 1 - core], core_in, one_s.at[2], one_r.at[2], core_dev)

    def tp_copy():
        return remote(tp_out.at[1 - tp], tp_in, one_s.at[3], one_r.at[3], tp_dev)

    def y_copies():
        return [
            remote(
                core_sum.at[:, :, :, pl.ds(pl.multiple_of(((row + i + 1) % 4) * 128, 128), 128)],
                y_in.at[i], y_s.at[i], y_r.at[i], y_devs[i],
            )
            for i in range(3)
        ]

    def project():
        own_a.wait()
        for i in range(7):
            got(a_in.at[source_spots[i]], a_r.at[i])
        uppers, lowers = [], []
        for two in range(4):
            upper, lower = swap_halves(a_in[2 * two], a_in[2 * two + 1])
            uppers.append(upper)
            lowers.append(lower)
        attn = jnp.concatenate(
            [jnp.concatenate(uppers, axis=1), jnp.concatenate(lowers, axis=1)], axis=0
        )
        for half in range(2):
            share = lax.dot_general(
                gf[half], attn, (((0,), (0,)), ((), ())), preferred_element_type=F32
            )
            wp[half * 4:(half + 1) * 4] = share.astype(BF).reshape(4, 4, 2, 32, 512)
        core_copy().start()
        weight = wf[...].reshape(2, 1024, 512)
        for half in range(2):
            share = lax.dot_general(
                attn, weight[half], (((1,), (1,)), ((), ())), preferred_element_type=F32
            )
            tp_out[half] = share.astype(BF)
        tp_copy().start()

    def add_core():
        got(core_in, one_r.at[2])
        core_sum[...] = (wp[:, :, core].astype(F32) + core_in[...].astype(F32)).astype(BF)
        for copy in y_copies():
            copy.start()

    def backward_step(step, carry):
        t = (spot + order(7 - step)) % 8
        backward_tile(t)
        for copy in part_copies(t):
            copy.start()

        @pl.when(step > 0)
        def _():
            earlier = (spot + order(8 - step)) % 8
            send_home(earlier)
            home_copy(earlier).start()

        @pl.when(step == PROJECT_STEP)
        def _():
            project()

        @pl.when(step == CORE_STEP)
        def _():
            add_core()

        return carry

    lax.fori_loop(0, 8, backward_step, 0)

    def pack_query(index, carry):
        rows = pl.ds(pl.multiple_of(index * 128, 128), 128)
        values = grad_q[rows, :] * HS ** -0.5
        dq_out[index] = jnp.where(low, values[:64], pltpu.roll(values[64:], HS, 1)).astype(BF)
        return carry

    lax.fori_loop(0, 8, pack_query, 0)
    own_dq = pltpu.make_async_copy(dq_out.at[spot], dq_in.at[spot], local_sem.at[7])
    own_dq.start()
    for i in range(7):
        send(dq_out.at[peer_spots[i]], dq_in.at[spot], dq_s.at[i], dq_r.at[i], peers[i])
    send_home(spot)
    own_dkv.start()

    got(tp_in, one_r.at[3])
    layer_ref[...] = (tp_out[tp].astype(F32) + tp_in[...].astype(F32)).astype(BF)

    for i in range(3):
        got(y_in.at[i], y_r.at[i])
    y_sum[...] = (
        (core_sum[:, :, :, w_cols].astype(F32) + y_in[0].astype(F32))
        + (y_in[1].astype(F32) + y_in[2].astype(F32))
    ).astype(BF)
    for i in range(3):
        send(y_sum.at[:, (member + i + 1) % 4], m_in.at[i], m_s.at[i], m_r.at[i], group[i])
    for i in range(3):
        got(m_in.at[i], m_r.at[i])
    m_sum[...] = (
        (y_sum[:, member].astype(F32) + m_in[0].astype(F32))
        + (m_in[1].astype(F32) + m_in[2].astype(F32))
    ).astype(BF)
    for i in range(7):
        send(m_sum.at[peer_spots[i]], s_in.at[i], s_s.at[i], s_r.at[i], peers[i])
    summed = m_sum[spot].astype(F32)
    for i in range(7):
        got(s_in.at[i], s_r.at[i])
        summed = summed + s_in[i].astype(F32)
    piece[...] = summed
    own_spot = gw_ref.at[w_rows, w_cols]
    own_piece = pltpu.make_async_copy(piece, own_spot, local_sem.at[8])
    own_piece.start()
    for i in range(7):
        send(piece, own_spot, d_s.at[i], d_r.at[i], dp_devs[i])

    own_dq.wait()
    own_dkv.wait()
    for i in range(7):
        got(dq_in.at[source_spots[i]], dq_r.at[i])
        got(dkv_in.at[source_spots[i]], dkv_r.at[source_spots[i]])
    own_piece.wait()
    for i in range(7):
        source = (dp + 7 - i) % 8
        got(
            gw_ref.at[
                pl.ds(pl.multiple_of((source % 2) * 32, 32), 32),
                pl.ds(pl.multiple_of((source // 2) * 128, 128), 128),
            ],
            d_r.at[i],
        )

    def settle(t, carry):
        for copy in forward_copies(t) + part_copies(t):
            copy.wait_send()

        @pl.when(t != spot)
        def _():
            home_copy(t).wait_send()

        return carry

    lax.fori_loop(0, 8, settle, 0)
    for copy in weight_copies() + grad_copies() + y_copies() + [half_copy(), core_copy(), tp_copy()]:
        copy.wait_send()
    for copy in sent:
        copy.wait_send()


def finish_kernel(layer_in, dq_in, dkv_in, gw_in, layer_ref, gq_ref, gk_ref, gv_ref, gw_ref):
    layer_ref[...] = layer_in[...]
    gw_ref[...] = gw_in[...]
    for pair in range(4):
        cols = slice(pair * 128, (pair + 1) * 128)
        upper, lower = swap_halves(dq_in[2 * pair], dq_in[2 * pair + 1])
        gq_ref[:64, cols] = upper
        gq_ref[64:, cols] = lower
        keys, values = swap_halves(dkv_in[2 * pair], dkv_in[2 * pair + 1])
        gk_ref[:, cols] = keys
        gv_ref[:, cols] = values


def like(shape, dtype=BF):
    return jax.ShapeDtypeStruct(shape, dtype)


def dma(*counts):
    return [pltpu.SemaphoreType.DMA((count,)) for count in counts]


def body(query_states, key_states, value_states, out_weight, grad_output, segment_table):
    vmem = pl.BlockSpec(memory_space=pltpu.VMEM)
    smem = pl.BlockSpec(memory_space=pltpu.SMEM)
    low = lambda *shape: pltpu.VMEM(shape, BF)
    wide = lambda *shape: pltpu.VMEM(shape, F32)
    layer, dq, dkv, gw = pl.pallas_call(
        sublayer_kernel,
        out_shape=(like((128, 1024)), like((8, 64, 128)), like((8, 128, 128)), like((64, 512), F32)),
        in_specs=[smem] + [vmem] * 5,
        out_specs=(vmem,) * 4,
        scratch_shapes=[
            low(8, 128, 128), low(8, 64, 128), low(8, 64, 128), low(8, 4, 128, 128),
            low(8, 4, 64, 512), low(2, 128, 1024), low(8, 64, 128), low(8, 64, 128),
            pltpu.VMEM((1024, 128), jnp.int32), low(1024, 128), low(1024, 128), wide(1024, 128),
            low(8, 1024, 512), wide(8, 1024, 128), wide(1024, 128), wide(1024, 128), wide(1024, 128),
            wide(1024, 128), wide(1024, 128), wide(1024, 128), wide(128, 512),
            low(8, 64, 128), low(8, 64, 128), low(8, 64, 128),
            low(8, 4, 128, 128), low(8, 3, 128, 128), low(8, 128, 128),
            low(2, 128, 1024), low(128, 1024), low(8, 4, 2, 32, 512), low(8, 4, 32, 512),
            low(8, 4, 32, 512), low(3, 8, 4, 32, 128), low(8, 4, 32, 128), low(3, 8, 32, 128),
            low(8, 32, 128), low(7, 32, 128), wide(32, 128),
            *dma(9, 7, 7, 7, 7, 7, 8, 24, 24, 3, 3, 3, 3, 7, 7),
            *dma(7, 7, 24, 24, 8, 8, 7, 7, 3, 3, 3, 3, 7, 7, 7, 7, 4, 4),
        ],
        compiler_params=pltpu.CompilerParams(
            collective_id=0, has_side_effects=True, vmem_limit_bytes=VMEM_LIMIT
        ),
        name="sublayer",
    )(
        segment_table[0], query_states[0], key_states[0], value_states[0], out_weight, grad_output[0]
    )
    outs = pl.pallas_call(
        finish_kernel,
        out_shape=(
            like((128, 1024)), like((128, 512)), like((128, 512)), like((128, 512)), like((64, 512), F32),
        ),
        in_specs=[vmem] * 4,
        out_specs=(vmem,) * 5,
        name="unpack",
    )(layer, dq, dkv, gw)
    layer, grad_q, grad_k, grad_v, grad_w = outs
    return (layer[None], grad_q[None], grad_k[None], grad_v[None], grad_w)


def solution(mesh):
    placed = (
        P("dp", "ctx", "tp"),
        P("dp", "ctx", "tp"),
        P("dp", "ctx", "tp"),
        P("ctx", "tp"),
        P("dp", "ctx", "tp"),
        P("dp", None, None),
    )
    return jax.shard_map(
        body,
        mesh=mesh,
        in_specs=placed,
        out_specs=(
            P("dp", "ctx", "tp"),
            P("dp", "ctx", "tp"),
            P("dp", "ctx", "tp"),
            P("dp", "ctx", "tp"),
            P("ctx", "tp"),
        ),
        check_vma=False,
    )
```

time: 989 us -> 135 us (0.14)
  waiting for transfers between devices: 770 us -> 0 us
  Pallas kernels: 0 us -> 133 us
  starting transfers between devices: 72.9 us -> 0 us
  matrix products: 57.8 us -> 0 us
  local copies, waits for them, and re-layouts: 30.5 us -> 1.25 us
  other arithmetic: 14.8 us -> 0 us
  blocking collectives: 14.4 us -> 0 us
  between operations: 14.3 us -> 0.65 us
  loops' own time: 12.7 us -> 0 us
    unnamed x5 -> x0, waiting for transfers between devices: 573 us -> none
    pallas_call x0 -> x2, Pallas kernels: none -> 133 us  [the longest x1 131 us: body(): pl.pallas_call(sublayer_kernel, out_shape=(like((128, 1024)), like((8, 64...]
    all_to_all x6 -> x0, starting transfers between devices: 59.3 us -> none  [the longest x1 18.5 us: body(): lax.all_to_all(to_heads(pair_local.reshape(tokens_here, heads_here * 2 *...]
    dot_general x87 -> x0, matrix products: 57.8 us -> none  [the longest x24 19.9 us: tile_scores(): lax.dot_general(query_rows, tile_keys, (((1,), (1,)), ((), ())), preferre...]
    psum x1 -> x0, waiting for transfers between devices: 54.4 us -> none  [body(): grad_weight = lax.psum(weight_part, 'dp').astype(jnp.float32)]
    all_gather x1 -> x0, waiting for transfers between devices: 48.3 us -> none  [body(): weight_full = lax.all_gather(out_weight, 'ctx', axis=0, tiled=True)]
    all_to_all x6 -> x0, waiting for transfers between devices: 43.2 us -> none  [the longest x1 18.9 us: body(): lax.all_to_all(to_heads(pair_local.reshape(tokens_here, heads_here * 2 *...]
    reduce_scatter x1 -> x0, waiting for transfers between devices: 27.1 us -> none  [body(): lax.psum_scatter(partial_out.astype(jnp.bfloat16), 'tp', scatter_dimensio...]
  transfers between devices with their start and end apart: 14 -> 0, of which waited for: 11 -> 0; matrix products, arithmetic and copies ran while one was open for 10% -> 0% of each run, Pallas kernels for 0% -> 0%
where the time goes in v2:
time: 135 us
  Pallas kernels  133 us (99%)
    pallas_call x1, Pallas kernels, body(): pl.pallas_call(sublayer_kernel, out_shape=(like((128, 1024)), like((8, 64...  131 us

profile of v2, /device:TPU:1, one launch (start us, length us, event | category | flops | bytes accessed | tf_op | source)
XLA Modules:
  0.0 135.0 jit_solution(4205918321328485997)
XLA Ops:
  0.6 0.0 copy-start
  0.6 0.7 copy-done
  1.3 0.6 copy.13
  1.9 131.0 %sublayer.1 = (bf16[128,1024]{1,0:T(8,128)(2,1)}, bf16[8,64,128]{2,1,0:T(8,128)(2,1)}, bf16[8,128,128]{2,1,0:T(8,128)(2,1)}, f32[64,512]{1,0:T(8,128)}) custom-call(s32[3,5]{1,0:T(4,128)} %bitcast.15, bf16[128,512]{1,0:T(8,128)(2,1)} %bitcast.12, bf16[128,512]{1,0:T(8,128)(2,1)} %bitcast.13, bf16[128,512]{1,0:T(8,128)(2,1)} %bitcast.14, ...), custom_call_target="tpu_custom_call" | custom-call | tf_op jit(solution)/shard_map/sublayer/pallas_call | solution.py:530
  132.9 2.1 %unpack.1 = (bf16[128,1024]{1,0:T(8,128)(2,1)}, bf16[128,512]{1,0:T(8,128)(2,1)}, bf16[128,512]{1,0:T(8,128)(2,1)}, bf16[128,512]{1,0:T(8,128)(2,1)}, f32[64,512]{1,0:T(8,128)}) custom-call(bf16[128,1024]{1,0:T(8,128)(2,1)} %get-tuple-element.14.layer_in, bf16[8,64,128]{2,1,0:T(8,128)(2,1)} %get-tuple-element.15.dq_in, ...), custom_call_target="tpu_custom_call" | custom-call | tf_op jit(solution)/shard_map/unpack/pallas_call | solution.py:556
Async XLA Ops:
  0.6 0.7 copy-start

commit v3 on v2

--- a/solution.py
+++ b/solution.py
@@ -15,10 +15,16 @@
 BF = jnp.bfloat16
 F32 = jnp.float32
 VMEM_LIMIT = 56 * 2**20
-W_HALF_STEP = 3
-W_DONE_STEP = 5
-PROJECT_STEP = 2
-CORE_STEP = 4
+FORWARD_ROWS = 1024
+BACKWARD_ROWS = 512
+AHEAD = 4
+RELAY = 2
+BEHIND = 2
+BEHIND_Z = 3
+SWAP_STEP = 4
+W_HALF_STEP = 6
+CORE_STEP = 0
+ROW_STEP = 4
 
 
 def swap_halves(first, second):
@@ -48,6 +54,14 @@
     return ctx, ctx // 4, ctx % 4, dp // 2, dp % 2, tp
 
 
+def flip_x(member):
+    return member + 1 - 2 * (member % 2)
+
+
+def flip_z(member):
+    return member + 2 - 4 * (member // 2)
+
+
 def greet(devices):
     barrier = pltpu.get_barrier_semaphore()
     for device in devices:
@@ -65,10 +79,10 @@
     layer_ref, dq_in, dkv_in, gw_ref,
     kv_out, q_out, qh, kv, wf, gf, g_out, gh,
     reach_ref, query, grad, both, probs, tops, top, total, out, base, delta, grad_q, acc,
-    a_out, a_in, dq_out, part, part_in, part_sum,
+    a_out, a_in, dq_out, part, part_in, part_sum, part_all,
     tp_out, tp_in, wp, core_in, core_sum, y_in, y_sum, m_in, m_sum, s_in, piece,
     local_sem, w_s, w_r, q_s, q_r, kv_s, kv_r, fwd_s, fwd_r, wm_s, wm_r, wy_s, wy_r, gh_s, gh_r,
-    a_s, a_r, part_s, part_r, dkv_s, dkv_r, dq_s, dq_r, y_s, y_r, m_s, m_r, s_s, s_r, d_s, d_r, one_s, one_r,
+    a_s, a_r, part_s, part_r, dkv_s, dkv_r, dq_s, dq_r, y_s, y_r, m_s, m_r, s_s, s_r, d_s, d_r, core_s, core_r, one_s, one_r,
 ):
     ctx, spot, member, row, core, tp = places()
     near_first = [1, 7, 2, 6, 3, 5, 4]
@@ -122,13 +136,20 @@
         send(q_out.at[peer_spots[i]], qh.at[spot], q_s.at[i], q_r.at[i], peers[i])
     for i in range(7):
         send(kv_out.at[peer_spots[i]], kv.at[spot, member], kv_s.at[i], kv_r.at[spot], peers[i])
-    send(g_ref, gf.at[tp], one_s.at[0], one_r.at[0], tp_dev)
+
+    x_member, z_member = flip_x(member), flip_z(member)
+    x_dev = {"ctx": spot * 4 + x_member}
+    z_dev = {"ctx": spot * 4 + z_member}
+
+    def share_copy(t, which, i, device):
+        slab = kv.at[t, which]
+        return remote(slab, slab, fwd_s.at[t * 3 + i], fwd_r.at[t * 3 + i], device)
 
     def forward_copies(t):
-        return [
-            remote(kv.at[t, member], kv.at[t, member], fwd_s.at[t * 3 + i], fwd_r.at[t * 3 + i], group[i])
-            for i in range(3)
-        ]
+        return [share_copy(t, member, 0, z_dev), share_copy(t, member, 1, x_dev)]
+
+    def relay_copy(t):
+        return share_copy(t, z_member, 2, x_dev)
 
     own_kv.wait()
     for copy in forward_copies(spot):
@@ -169,14 +190,14 @@
             low, pltpu.roll(packed, HS, 1), 0.0
         ).astype(BF)
 
-    def first_pair(t):
-        return jnp.maximum(4 * t - 5 - member, 0) // 8
+    def first_group(t, row_count):
+        return jnp.maximum(4 * t - 5 - member, 0) // (row_count // 32)
 
     def forward_tile(t):
         tile = kv[t].reshape(TILE, 128)
 
-        def pair(index, carry):
-            rows = pl.ds(pl.multiple_of(index * 256, 256), 256)
+        def group_of(index, carry):
+            rows = pl.ds(pl.multiple_of(index * FORWARD_ROWS, FORWARD_ROWS), FORWARD_ROWS)
             scores = lax.dot_general(
                 query[rows, :], tile, (((1,), (1,)), ((), ())), preferred_element_type=F32
             )
@@ -200,7 +221,7 @@
             tops[t, rows, :] = now
             return carry
 
-        lax.fori_loop(first_pair(t), 4, pair, 0)
+        lax.fori_loop(first_group(t, FORWARD_ROWS), 1024 // FORWARD_ROWS, group_of, 0)
 
     w_part = wf.at[:, :, w_rows, w_cols]
     w_half = wf.at[:, :, w_rows, :]
@@ -217,20 +238,30 @@
             for i in range(7)
         ]
 
+    def swap_copy():
+        return remote(g_ref, gf.at[tp], one_s.at[0], one_r.at[0], tp_dev)
+
     own_gh = pltpu.make_async_copy(g_out.at[spot], gh.at[spot], local_sem.at[4])
+
+    def pass_on(step):
+        t = (spot + order(step)) % 8
+        got(kv.at[t, member], kv_r.at[t])
+        for copy in forward_copies(t):
+            copy.start()
 
     def forward_step(step, carry):
         t = (spot + order(step)) % 8
 
-        @pl.when(step < 7)
-        def _():
-            later = (spot + order(step + 1)) % 8
-            got(kv.at[later, member], kv_r.at[later])
-            for copy in forward_copies(later):
-                copy.start()
-
-        for i in range(3):
-            got(kv.at[t, (member + 3 - i) % 4], fwd_r.at[t * 3 + i])
+        @pl.when(step < 8 - AHEAD)
+        def _():
+            pass_on(step + AHEAD)
+
+        @pl.when(step < 8 - RELAY)
+        def _():
+            relay(step + RELAY)
+
+        got(kv.at[t, x_member], fwd_r.at[t * 3 + 1])
+        got(kv.at[t, flip_z(x_member)], fwd_r.at[t * 3 + 2])
         forward_tile(t)
 
         @pl.when(step == 0)
@@ -247,26 +278,21 @@
                 got(wf.at[:, :, w_rows, pl.ds(pl.multiple_of(from_row * 128, 128), 128)], wy_r.at[i])
             half_copy().start()
 
-        @pl.when(step == W_DONE_STEP)
-        def _():
-            got(wf.at[:, :, pl.ds(pl.multiple_of(32 - core * 32, 32), 32), :], one_r.at[1])
-            own_g.wait()
-            got(gf.at[1 - tp], one_r.at[0])
-            weight = wf[...].reshape(2048, 512)
-            grad_attn = jnp.dot(gf[0], weight[:1024], preferred_element_type=F32)
-            grad_attn += jnp.dot(gf[1], weight[1024:], preferred_element_type=F32)
-            grad_attn = grad_attn.astype(BF)
-            for two in range(4):
-                cols = slice(two * 128, (two + 1) * 128)
-                even, odd = swap_halves(grad_attn[:64, cols], grad_attn[64:, cols])
-                g_out[2 * two] = even
-                g_out[2 * two + 1] = odd
-            own_gh.start()
-            for copy in grad_copies():
-                copy.start()
+        @pl.when(step == SWAP_STEP)
+        def _():
+            swap_copy().start()
 
         return carry
 
+    def relay(step):
+        t = (spot + order(step)) % 8
+        got(kv.at[t, z_member], fwd_r.at[t * 3])
+        relay_copy(t).start()
+
+    for step in range(1, AHEAD):
+        pass_on(step)
+    for step in range(RELAY):
+        relay(step)
     lax.fori_loop(0, 8, forward_step, 0)
 
     def finish(index, carry):
@@ -283,6 +309,77 @@
     own_a.start()
     for i in range(7):
         send(a_out.at[peer_spots[i]], a_in.at[spot], a_s.at[i], a_r.at[i], peers[i])
+
+    got(wf.at[:, :, pl.ds(pl.multiple_of(32 - core * 32, 32), 32), :], one_r.at[1])
+    own_g.wait()
+    got(gf.at[1 - tp], one_r.at[0])
+    weight = wf[...].reshape(2048, 512)
+    grad_attn = jnp.dot(gf[0], weight[:1024], preferred_element_type=F32)
+    grad_attn += jnp.dot(gf[1], weight[1024:], preferred_element_type=F32)
+    grad_attn = grad_attn.astype(BF)
+    for two in range(4):
+        cols = slice(two * 128, (two + 1) * 128)
+        even, odd = swap_halves(grad_attn[:64, cols], grad_attn[64:, cols])
+        g_out[2 * two] = even
+        g_out[2 * two + 1] = odd
+    own_gh.start()
+    for copy in grad_copies():
+        copy.start()
+
+    def core_copy(half):
+        spots = pl.ds(half * 4, 4)
+        return remote(
+            wp.at[spots, :, 1 - core], core_in.at[spots], core_s.at[half], core_r.at[half], core_dev
+        )
+
+    def tp_copy():
+        return remote(tp_out.at[1 - tp], tp_in, one_s.at[3], one_r.at[3], tp_dev)
+
+    def y_copies(half):
+        spots = pl.ds(half * 4, 4)
+        return [
+            remote(
+                core_sum.at[spots, :, :, pl.ds(pl.multiple_of(((row + i + 1) % 4) * 128, 128), 128)],
+                y_in.at[i, spots], y_s.at[half * 3 + i], y_r.at[half * 3 + i], y_devs[i],
+            )
+            for i in range(3)
+        ]
+
+    def project():
+        own_a.wait()
+        for i in range(7):
+            got(a_in.at[source_spots[i]], a_r.at[i])
+        uppers, lowers = [], []
+        for two in range(4):
+            upper, lower = swap_halves(a_in[2 * two], a_in[2 * two + 1])
+            uppers.append(upper)
+            lowers.append(lower)
+        attn = jnp.concatenate(
+            [jnp.concatenate(uppers, axis=1), jnp.concatenate(lowers, axis=1)], axis=0
+        )
+        for half in range(2):
+            share = lax.dot_general(
+                gf[half], attn, (((0,), (0,)), ((), ())), preferred_element_type=F32
+            )
+            wp[half * 4:(half + 1) * 4] = share.astype(BF).reshape(4, 4, 2, 32, 512)
+            core_copy(half).start()
+        weight = wf[...].reshape(2, 1024, 512)
+        for half in range(2):
+            share = lax.dot_general(
+                attn, weight[half], (((1,), (1,)), ((), ())), preferred_element_type=F32
+            )
+            tp_out[half] = share.astype(BF)
+        tp_copy().start()
+
+    def add_core():
+        for half in range(2):
+            spots = pl.ds(half * 4, 4)
+            got(core_in.at[spots], core_r.at[half])
+            core_sum[spots] = (wp[spots, :, core].astype(F32) + core_in[spots].astype(F32)).astype(BF)
+            for copy in y_copies(half):
+                copy.start()
+
+    project()
 
     own_gh.wait()
     for i in range(7):
@@ -307,8 +404,8 @@
         tile = kv[t].reshape(TILE, 128)
         acc[...] = jnp.zeros_like(acc)
 
-        def pair(index, carry):
-            rows = pl.ds(pl.multiple_of(index * 256, 256), 256)
+        def group_of(index, carry):
+            rows = pl.ds(pl.multiple_of(index * BACKWARD_ROWS, BACKWARD_ROWS), BACKWARD_ROWS)
             factor = jnp.exp(tops[t, rows, :] - base[rows, :])
             turned = jnp.transpose(both[rows, :] * factor).astype(BF)
             grad_probs = lax.dot_general(
@@ -331,73 +428,55 @@
             grad_q[rows, :] += factor * jnp.dot(grad_scores, tile, preferred_element_type=F32)
             return carry
 
-        lax.fori_loop(first_pair(t), 4, pair, 0)
+        lax.fori_loop(first_group(t, BACKWARD_ROWS), 1024 // BACKWARD_ROWS, group_of, 0)
         part[t] = jnp.transpose(acc[...]).astype(BF).reshape(4, 128, 128)
 
     def part_copies(t):
         return [
-            remote(part.at[t, (member + i + 1) % 4], part_in.at[t, i], part_s.at[t * 3 + i], part_r.at[t * 3 + i], group[i])
+            remote(part.at[t, x_member], part_in.at[t, 0], part_s.at[t * 3], part_r.at[t * 3], x_dev),
+            remote(
+                part.at[t, flip_z(x_member)], part_in.at[t, 1],
+                part_s.at[t * 3 + 1], part_r.at[t * 3 + 1], x_dev,
+            ),
+        ]
+
+    def part_z_copy(t):
+        return remote(
+            part_sum.at[t], part_in.at[t, 2], part_s.at[t * 3 + 2], part_r.at[t * 3 + 2], z_dev
+        )
+
+    def home_copy(t):
+        return remote(part_all.at[t], dkv_in.at[spot], dkv_s.at[t], dkv_r.at[spot], {"ctx": t * 4 + member})
+
+    own_dkv = pltpu.make_async_copy(part_all.at[spot], dkv_in.at[spot], local_sem.at[6])
+
+    def send_z(t):
+        for i in range(2):
+            got(part_in.at[t, i], part_r.at[t * 3 + i])
+        part_sum[t] = (part[t, z_member].astype(F32) + part_in[t, 1].astype(F32)).astype(BF)
+        part_z_copy(t).start()
+
+    def send_home(t):
+        got(part_in.at[t, 2], part_r.at[t * 3 + 2])
+        part_all[t] = (
+            part[t, member].astype(F32) + part_in[t, 0].astype(F32) + part_in[t, 2].astype(F32)
+        ).astype(BF)
+
+    def group_copies():
+        return [
+            remote(y_sum.at[:, (member + i + 1) % 4], m_in.at[i], m_s.at[i], m_r.at[i], group[i])
             for i in range(3)
         ]
 
-    def home_copy(t):
-        return remote(part_sum.at[t], dkv_in.at[spot], dkv_s.at[t], dkv_r.at[spot], {"ctx": t * 4 + member})
-
-    own_dkv = pltpu.make_async_copy(part_sum.at[spot], dkv_in.at[spot], local_sem.at[6])
-
-    def send_home(t):
-        for i in range(3):
-            got(part_in.at[t, i], part_r.at[t * 3 + i])
-        part_sum[t] = (
-            (part[t, member].astype(F32) + part_in[t, 0].astype(F32))
-            + (part_in[t, 1].astype(F32) + part_in[t, 2].astype(F32))
+    def add_rows():
+        for half in range(2):
+            for i in range(3):
+                got(y_in.at[i, pl.ds(half * 4, 4)], y_r.at[half * 3 + i])
+        y_sum[...] = (
+            (core_sum[:, :, :, w_cols].astype(F32) + y_in[0].astype(F32))
+            + (y_in[1].astype(F32) + y_in[2].astype(F32))
         ).astype(BF)
-
-    def core_copy():
-        return remote(wp.at[:, :, 1 - core], core_in, one_s.at[2], one_r.at[2], core_dev)
-
-    def tp_copy():
-        return remote(tp_out.at[1 - tp], tp_in, one_s.at[3], one_r.at[3], tp_dev)
-
-    def y_copies():
-        return [
-            remote(
-                core_sum.at[:, :, :, pl.ds(pl.multiple_of(((row + i + 1) % 4) * 128, 128), 128)],
-                y_in.at[i], y_s.at[i], y_r.at[i], y_devs[i],
-            )
-            for i in range(3)
-        ]
-
-    def project():
-        own_a.wait()
-        for i in range(7):
-            got(a_in.at[source_spots[i]], a_r.at[i])
-        uppers, lowers = [], []
-        for two in range(4):
-            upper, lower = swap_halves(a_in[2 * two], a_in[2 * two + 1])
-            uppers.append(upper)
-            lowers.append(lower)
-        attn = jnp.concatenate(
-            [jnp.concatenate(uppers, axis=1), jnp.concatenate(lowers, axis=1)], axis=0
-        )
-        for half in range(2):
-            share = lax.dot_general(
-                gf[half], attn, (((0,), (0,)), ((), ())), preferred_element_type=F32
-            )
-            wp[half * 4:(half + 1) * 4] = share.astype(BF).reshape(4, 4, 2, 32, 512)
-        core_copy().start()
-        weight = wf[...].reshape(2, 1024, 512)
-        for half in range(2):
-            share = lax.dot_general(
-                attn, weight[half], (((1,), (1,)), ((), ())), preferred_element_type=F32
-            )
-            tp_out[half] = share.astype(BF)
-        tp_copy().start()
-
-    def add_core():
-        got(core_in, one_r.at[2])
-        core_sum[...] = (wp[:, :, core].astype(F32) + core_in[...].astype(F32)).astype(BF)
-        for copy in y_copies():
+        for copy in group_copies():
             copy.start()
 
     def backward_step(step, carry):
@@ -406,49 +485,28 @@
         for copy in part_copies(t):
             copy.start()
 
-        @pl.when(step > 0)
-        def _():
-            earlier = (spot + order(8 - step)) % 8
+        @pl.when(step >= BEHIND)
+        def _():
+            send_z((spot + order(7 + BEHIND - step)) % 8)
+
+        @pl.when(step >= BEHIND_Z)
+        def _():
+            earlier = (spot + order(7 + BEHIND_Z - step)) % 8
             send_home(earlier)
             home_copy(earlier).start()
 
-        @pl.when(step == PROJECT_STEP)
-        def _():
-            project()
-
         @pl.when(step == CORE_STEP)
         def _():
             add_core()
 
+        @pl.when(step == ROW_STEP)
+        def _():
+            add_rows()
+
         return carry
 
     lax.fori_loop(0, 8, backward_step, 0)
 
-    def pack_query(index, carry):
-        rows = pl.ds(pl.multiple_of(index * 128, 128), 128)
-        values = grad_q[rows, :] * HS ** -0.5
-        dq_out[index] = jnp.where(low, values[:64], pltpu.roll(values[64:], HS, 1)).astype(BF)
-        return carry
-
-    lax.fori_loop(0, 8, pack_query, 0)
-    own_dq = pltpu.make_async_copy(dq_out.at[spot], dq_in.at[spot], local_sem.at[7])
-    own_dq.start()
-    for i in range(7):
-        send(dq_out.at[peer_spots[i]], dq_in.at[spot], dq_s.at[i], dq_r.at[i], peers[i])
-    send_home(spot)
-    own_dkv.start()
-
-    got(tp_in, one_r.at[3])
-    layer_ref[...] = (tp_out[tp].astype(F32) + tp_in[...].astype(F32)).astype(BF)
-
-    for i in range(3):
-        got(y_in.at[i], y_r.at[i])
-    y_sum[...] = (
-        (core_sum[:, :, :, w_cols].astype(F32) + y_in[0].astype(F32))
-        + (y_in[1].astype(F32) + y_in[2].astype(F32))
-    ).astype(BF)
-    for i in range(3):
-        send(y_sum.at[:, (member + i + 1) % 4], m_in.at[i], m_s.at[i], m_r.at[i], group[i])
     for i in range(3):
         got(m_in.at[i], m_r.at[i])
     m_sum[...] = (
@@ -457,6 +515,29 @@
     ).astype(BF)
     for i in range(7):
         send(m_sum.at[peer_spots[i]], s_in.at[i], s_s.at[i], s_r.at[i], peers[i])
+    def pack_query(index, carry):
+        rows = pl.ds(pl.multiple_of(index * 128, 128), 128)
+        values = grad_q[rows, :] * HS ** -0.5
+        dq_out[index] = jnp.where(low, values[:64], pltpu.roll(values[64:], HS, 1)).astype(BF)
+        return carry
+
+    lax.fori_loop(0, 8, pack_query, 0)
+    own_dq = pltpu.make_async_copy(dq_out.at[spot], dq_in.at[spot], local_sem.at[7])
+    own_dq.start()
+    for i in range(7):
+        send(dq_out.at[peer_spots[i]], dq_in.at[spot], dq_s.at[i], dq_r.at[i], peers[i])
+    for step in range(8 - BEHIND, 8):
+        send_z((spot + order(7 - step)) % 8)
+    for step in range(8 - BEHIND_Z, 7):
+        earlier = (spot + order(7 - step)) % 8
+        send_home(earlier)
+        home_copy(earlier).start()
+    send_home(spot)
+    own_dkv.start()
+
+    got(tp_in, one_r.at[3])
+    layer_ref[...] = (tp_out[tp].astype(F32) + tp_in[...].astype(F32)).astype(BF)
+
     summed = m_sum[spot].astype(F32)
     for i in range(7):
         got(s_in.at[i], s_r.at[i])
@@ -485,7 +566,7 @@
         )
 
     def settle(t, carry):
-        for copy in forward_copies(t) + part_copies(t):
+        for copy in forward_copies(t) + part_copies(t) + [relay_copy(t), part_z_copy(t)]:
             copy.wait_send()
 
         @pl.when(t != spot)
@@ -495,9 +576,9 @@
         return carry
 
     lax.fori_loop(0, 8, settle, 0)
-    for copy in weight_copies() + grad_copies() + y_copies() + [half_copy(), core_copy(), tp_copy()]:
+    for copy in weight_copies() + grad_copies() + y_copies(0) + y_copies(1) + group_copies() + [half_copy(), tp_copy(), swap_copy()]:
         copy.wait_send()
-    for copy in sent:
+    for copy in [core_copy(0), core_copy(1)] + sent:
         copy.wait_send()
 
 
@@ -539,12 +620,12 @@
             low(8, 1024, 512), wide(8, 1024, 128), wide(1024, 128), wide(1024, 128), wide(1024, 128),
             wide(1024, 128), wide(1024, 128), wide(1024, 128), wide(128, 512),
             low(8, 64, 128), low(8, 64, 128), low(8, 64, 128),
-            low(8, 4, 128, 128), low(8, 3, 128, 128), low(8, 128, 128),
+            low(8, 4, 128, 128), low(8, 3, 128, 128), low(8, 128, 128), low(8, 128, 128),
             low(2, 128, 1024), low(128, 1024), low(8, 4, 2, 32, 512), low(8, 4, 32, 512),
             low(8, 4, 32, 512), low(3, 8, 4, 32, 128), low(8, 4, 32, 128), low(3, 8, 32, 128),
             low(8, 32, 128), low(7, 32, 128), wide(32, 128),
             *dma(9, 7, 7, 7, 7, 7, 8, 24, 24, 3, 3, 3, 3, 7, 7),
-            *dma(7, 7, 24, 24, 8, 8, 7, 7, 3, 3, 3, 3, 7, 7, 7, 7, 4, 4),
+            *dma(7, 7, 24, 24, 8, 8, 7, 7, 6, 6, 3, 3, 7, 7, 7, 7, 2, 2, 4, 4),
         ],
         compiler_params=pltpu.CompilerParams(
             collective_id=0, has_side_effects=True, vmem_limit_bytes=VMEM_LIMIT

time: 135 us -> 130 us (0.963)
  Pallas kernels: 133 us -> 128 us
    pallas_call x1, Pallas kernels: 131 us -> 126 us  [body(): pl.pallas_call(sublayer_kernel, out_shape=(like((128, 1024)), like((8, 64...]
where the time goes in v3:
time: 130 us
  Pallas kernels  128 us (98%)
    pallas_call x1, Pallas kernels, body(): pl.pallas_call(sublayer_kernel, out_shape=(like((128, 1024)), like((8, 64...  126 us

profile of v3, /device:TPU:1, one launch (start us, length us, event | category | flops | bytes accessed | tf_op | source)
XLA Modules:
  0.0 130.1 jit_solution(7375850584363287804)
XLA Ops:
  0.6 0.0 copy-start
  0.6 0.7 copy-done
  1.3 0.6 copy.13
  1.9 126.1 %sublayer.1 = (bf16[128,1024]{1,0:T(8,128)(2,1)}, bf16[8,64,128]{2,1,0:T(8,128)(2,1)}, bf16[8,128,128]{2,1,0:T(8,128)(2,1)}, f32[64,512]{1,0:T(8,128)}) custom-call(s32[3,5]{1,0:T(4,128)} %bitcast.15, bf16[128,512]{1,0:T(8,128)(2,1)} %bitcast.12, bf16[128,512]{1,0:T(8,128)(2,1)} %bitcast.13, bf16[128,512]{1,0:T(8,128)(2,1)} %bitcast.14, ...), custom_call_target="tpu_custom_call" | custom-call | tf_op jit(solution)/shard_map/sublayer/pallas_call | solution.py:611
  128.0 2.1 %unpack.1 = (bf16[128,1024]{1,0:T(8,128)(2,1)}, bf16[128,512]{1,0:T(8,128)(2,1)}, bf16[128,512]{1,0:T(8,128)(2,1)}, bf16[128,512]{1,0:T(8,128)(2,1)}, f32[64,512]{1,0:T(8,128)}) custom-call(bf16[128,1024]{1,0:T(8,128)(2,1)} %get-tuple-element.14.layer_in, bf16[8,64,128]{2,1,0:T(8,128)(2,1)} %get-tuple-element.15.dq_in, ...), custom_call_target="tpu_custom_call" | custom-call | tf_op jit(solution)/shard_map/unpack/pallas_call | solution.py:637
Async XLA Ops:
  0.6 0.7 copy-start

commit v4 on v3

--- a/solution.py
+++ b/solution.py
@@ -345,24 +345,30 @@
             for i in range(3)
         ]
 
-    def project():
-        own_a.wait()
-        for i in range(7):
-            got(a_in.at[source_spots[i]], a_r.at[i])
+    def attn_here():
         uppers, lowers = [], []
         for two in range(4):
             upper, lower = swap_halves(a_in[2 * two], a_in[2 * two + 1])
             uppers.append(upper)
             lowers.append(lower)
-        attn = jnp.concatenate(
+        return jnp.concatenate(
             [jnp.concatenate(uppers, axis=1), jnp.concatenate(lowers, axis=1)], axis=0
         )
+
+    def weigh():
+        own_a.wait()
+        for i in range(7):
+            got(a_in.at[source_spots[i]], a_r.at[i])
+        attn = attn_here()
         for half in range(2):
             share = lax.dot_general(
                 gf[half], attn, (((0,), (0,)), ((), ())), preferred_element_type=F32
             )
             wp[half * 4:(half + 1) * 4] = share.astype(BF).reshape(4, 4, 2, 32, 512)
             core_copy(half).start()
+
+    def project():
+        attn = attn_here()
         weight = wf[...].reshape(2, 1024, 512)
         for half in range(2):
             share = lax.dot_general(
@@ -379,7 +385,7 @@
             for copy in y_copies(half):
                 copy.start()
 
-    project()
+    weigh()
 
     own_gh.wait()
     for i in range(7):
@@ -535,9 +541,7 @@
     send_home(spot)
     own_dkv.start()
 
-    got(tp_in, one_r.at[3])
-    layer_ref[...] = (tp_out[tp].astype(F32) + tp_in[...].astype(F32)).astype(BF)
-
+    project()
     summed = m_sum[spot].astype(F32)
     for i in range(7):
         got(s_in.at[i], s_r.at[i])
@@ -548,6 +552,9 @@
     own_piece.start()
     for i in range(7):
         send(piece, own_spot, d_s.at[i], d_r.at[i], dp_devs[i])
+
+    got(tp_in, one_r.at[3])
+    layer_ref[...] = (tp_out[tp].astype(F32) + tp_in[...].astype(F32)).astype(BF)
 
     own_dq.wait()
     own_dkv.wait()

time: 130 us -> 129 us (level)
  no operation moved by 1% of the time
where the time goes in v4:
time: 129 us
  Pallas kernels  127 us (98%)
    pallas_call x1, Pallas kernels, body(): pl.pallas_call(sublayer_kernel, out_shape=(like((128, 1024)), like((8, 64...  125 us

profile of v4, /device:TPU:1, one launch (start us, length us, event | category | flops | bytes accessed | tf_op | source)
XLA Modules:
  0.0 129.1 jit_solution(15809189103575305763)
XLA Ops:
  0.6 0.0 copy-start
  0.6 0.7 copy-done
  1.3 0.6 copy.13
  1.9 125.0 %sublayer.1 = (bf16[128,1024]{1,0:T(8,128)(2,1)}, bf16[8,64,128]{2,1,0:T(8,128)(2,1)}, bf16[8,128,128]{2,1,0:T(8,128)(2,1)}, f32[64,512]{1,0:T(8,128)}) custom-call(s32[3,5]{1,0:T(4,128)} %bitcast.15, bf16[128,512]{1,0:T(8,128)(2,1)} %bitcast.12, bf16[128,512]{1,0:T(8,128)(2,1)} %bitcast.13, bf16[128,512]{1,0:T(8,128)(2,1)} %bitcast.14, ...), custom_call_target="tpu_custom_call" | custom-call | tf_op jit(solution)/shard_map/sublayer/pallas_call | solution.py:618
  126.9 2.1 %unpack.1 = (bf16[128,1024]{1,0:T(8,128)(2,1)}, bf16[128,512]{1,0:T(8,128)(2,1)}, bf16[128,512]{1,0:T(8,128)(2,1)}, bf16[128,512]{1,0:T(8,128)(2,1)}, f32[64,512]{1,0:T(8,128)}) custom-call(bf16[128,1024]{1,0:T(8,128)(2,1)} %get-tuple-element.14.layer_in, bf16[8,64,128]{2,1,0:T(8,128)(2,1)} %get-tuple-element.15.dq_in, ...), custom_call_target="tpu_custom_call" | custom-call | tf_op jit(solution)/shard_map/unpack/pallas_call | solution.py:644
Async XLA Ops:
  0.6 0.7 copy-start
